TPU v7x, 256 devices: a whole 4x4x8 slice. The times are simulated.
256 devices in a mesh: ctx: 64 (over x, z, core), tp: 4 (over y).
Axes of the slice: x: 4, y: 4, z: 8, core: 2. Of those that a mesh axis runs over, the one named last changes fastest.
Arguments:
- hidden: bfloat16 [28672, 8192], P('ctx', 'tp'), may hold values from -14 to 14
- query_rows: bfloat16 [512, 4096], P('ctx', 'tp'), may hold values from -35 to 35
- query_weight: bfloat16 [8192, 4096], P('ctx', 'tp'), may hold values from -0.125 to 0.125
- key_weight: bfloat16 [8192, 512], P('ctx', 'tp'), may hold values from -0.0625 to 0.0625
- value_weight: bfloat16 [8192, 512], P('ctx', 'tp'), may hold values from -0.0625 to 0.0625
- query_down: bfloat16 [8192, 128], P('tp'), may hold values from -0.0625 to 0.0625
- value_down: bfloat16 [8192, 128], P('tp'), may hold values from -0.0625 to 0.0625
- query_up: bfloat16 [8, 16, 4096], P(None, None, 'tp'), may hold values from -1.5 to 1.5
- value_up: bfloat16 [8, 16, 512], P(None, None, 'tp'), may hold values from -1.5 to 1.5
- block_order: int32 [64], replicated, may hold values from 0 to 63, each once
- tenant: int32 [64], replicated, may hold values from 0 to 7
Outputs:
- context_out: bfloat16 [28672, 4096], P('ctx', 'tp')
- answer: bfloat16 [512, 4096], P('ctx', 'tp')
All inputs are finite; a program needn't handle non-finite values.
Results may differ from a plain program's by a relative error of at most 0.028.
The roundings to bfloat16 on the way count: a program that leaves them out, or rounds other values in their place, can miss the bound.
Values may be sent and summed in bfloat16 or wider, within the bound.
No kernel may reach another device: no remote copies, remote signals or barrier semaphores. Data moves between devices by JAX's collectives and lax.ppermute only.
A program may use at most 128 MiB of HBM per device.

v0:
```python
import functools

import jax
import jax.numpy as jnp
from jax import lax
from jax.experimental import pallas as pl
from jax.experimental.pallas import tpu as pltpu
from jax.sharding import PartitionSpec as P

HEAD = 128
RANK = 16
XS, ZS, YS = 4, 8, 4
CORE, Z1, Z2, Z4, X1, X2 = 1, 2, 4, 8, 16, 32
LINE_SENT = 256
LINE = 192
AROUND, BLOCK_ID, CORE_AT, PLACE_X, OWNER, FLAGS = 0, 1, 2, 3, 4, 5
ROWS = 448
VMEM = 32 * 1024 * 1024
BF = jnp.bfloat16
F32 = jnp.float32

rope_base = 500000.0
masked = -1e30
scale = HEAD ** (-0.5)
power = scale * 1.4426950408889634


def place(x, z, core):
    return (x % XS) * 16 + (z % ZS) * 2 + core


def ctx_move(value, dx=0, dz=0, swap=False):
    pairs = []
    for x in range(XS):
        for z in range(ZS):
            for core in range(2):
                pairs.append((place(x, z, core), place(x + dx, z + dz, 1 - core if swap else core)))
    return lax.ppermute(value, "ctx", pairs)


def ctx_flip(value, bit):
    return lax.ppermute(value, "ctx", [(i, i ^ bit) for i in range(64)])


def swap_core(value):
    return ctx_move(value, swap=True)


def gather_z(value):
    lines = [[place(x, z, core) for z in range(ZS)] for x in range(XS) for core in range(2)]
    return lax.all_gather(value, "ctx", axis_index_groups=lines, axis=0, tiled=True)


def move_y(value, dy):
    return lax.ppermute(value, "tp", [(y, (y + dy) % YS) for y in range(YS)])


def ring(piece, count, forward, backward):
    pieces = [None] * count
    pieces[0] = piece
    ahead = behind = piece
    for step in range(1, count // 2):
        ahead, behind = forward(ahead), backward(behind)
        pieces[step], pieces[count - step] = ahead, behind
    half = piece.shape[0] // 2
    pieces[count // 2] = (forward(ahead[:half]), backward(behind[half:]))
    return pieces


def ordered(pieces, me):
    count = len(pieces)
    buffer = jnp.zeros((count,) + pieces[0].shape, pieces[0].dtype)
    zeros = (0,) * (pieces[0].ndim - 1)
    for back, piece in enumerate(pieces):
        at = lax.rem(me - back + count, count)
        if isinstance(piece, tuple):
            low, high = piece
            buffer = lax.dynamic_update_slice(buffer, low[None], (at, 0) + zeros)
            buffer = lax.dynamic_update_slice(buffer, high[None], (at, low.shape[0]) + zeros)
        else:
            buffer = lax.dynamic_update_slice(buffer, piece[None], (at, 0) + zeros)
    return buffer


def call(kernel, flops, moved, exps=0, **kw):
    return pl.pallas_call(
        kernel,
        compiler_params=pltpu.CompilerParams(vmem_limit_bytes=VMEM),
        cost_estimate=pl.CostEstimate(flops=flops, bytes_accessed=moved, transcendentals=exps),
        **kw,
    )


def parity_kernel(core_ref, hidden_ref, mine_ref, theirs_ref):
    first = core_ref[0] == 0
    for block in range(8):
        even = hidden_ref[:, block * 256 : block * 256 + 128]
        odd = hidden_ref[:, block * 256 + 128 : block * 256 + 256]
        mine_ref[:, block * 128 : block * 128 + 128] = jnp.where(first, even, odd)
        theirs_ref[:, block * 128 : block * 128 + 128] = jnp.where(first, odd, even)


def split_parity(core, hidden):
    shape = jax.ShapeDtypeStruct((ROWS, 1024), BF)
    return call(
        parity_kernel,
        0,
        4 * ROWS * 2048,
        out_shape=(shape, shape),
        in_specs=[pl.BlockSpec(memory_space=pltpu.SMEM), pl.BlockSpec(memory_space=pltpu.VMEM)],
        out_specs=(pl.BlockSpec(memory_space=pltpu.VMEM),) * 2,
    )(core.reshape(1), hidden)


def low_kernel(number_ref, hidden_ref, query_ref, value_ref, out_ref):
    shift = number_ref[OWNER] * RANK
    low_q = jnp.dot(hidden_ref[...], query_ref[...], preferred_element_type=F32)
    low_v = jnp.dot(hidden_ref[...], value_ref[...], preferred_element_type=F32)
    low_q = pltpu.roll(low_q, lax.rem(128 - shift, 128), 1)
    low_v = pltpu.roll(low_v, lax.rem(128 + RANK - shift, 128), 1)
    lane = lax.broadcasted_iota(jnp.int32, low_q.shape, 1)
    out_ref[...] = jnp.where(lane < RANK, low_q, low_v).T[: 2 * RANK]


def low_parts(numbers, hidden, query_down, value_down):
    vmem = pl.BlockSpec(memory_space=pltpu.VMEM)
    return call(
        low_kernel,
        2 * ROWS * 2048 * 256,
        2 * 2048 * (ROWS + 256),
        out_shape=jax.ShapeDtypeStruct((2 * RANK, ROWS), F32),
        in_specs=[pl.BlockSpec(memory_space=pltpu.SMEM)] + [vmem] * 3,
        out_specs=vmem,
    )(numbers, hidden, query_down, value_down)


def both(step, own_refs, other_refs):
    return jnp.concatenate([own_refs[step][...], other_refs[(YS - step) % YS][...]], axis=0)


def project_kernel(number_ref, *refs):
    own_refs, other_refs, weight_ref, own_out, other_out = refs[:4], refs[4:8], refs[8], refs[9], refs[10]
    for tile in range(own_out.shape[1] // 256):
        cols = slice(tile * 256, tile * 256 + 256)
        sums = None
        for step in range(YS):
            at = lax.rem(number_ref[AROUND] + step, YS)
            if weight_ref.shape[0] == XS:
                blocks = [weight_ref[at, block, :128, cols] for block in range(ZS)]
            else:
                blocks = [weight_ref[block, at, :, cols] for block in range(ZS)]
            product = jnp.dot(
                both(step, own_refs, other_refs), jnp.concatenate(blocks, axis=0), preferred_element_type=F32
            )
            sums = product if sums is None else sums + product
        own_out[:, cols] = sums[:ROWS]
        other_out[:, cols] = sums[ROWS:]


def project(numbers, own, other, weight):
    cols = weight.shape[-1]
    out = jax.ShapeDtypeStruct((ROWS, cols), F32)
    vmem = pl.BlockSpec(memory_space=pltpu.VMEM)
    return call(
        project_kernel,
        4 * ROWS * 4096 * cols,
        2 * 4096 * (2 * ROWS + cols) + 8 * ROWS * cols,
        out_shape=(out, out),
        in_specs=[pl.BlockSpec(memory_space=pltpu.SMEM)] + [vmem] * 9,
        out_specs=(vmem, vmem),
    )(numbers, *own, *other, weight)


def turn(values, cosine, sine):
    return values * cosine + pltpu.roll(values, HEAD // 2, 1) * sine


def keys_kernel(own_ref, got_ref, lift_ref, cos_ref, sin_ref, out_ref):
    keys = own_ref[:, :HEAD] + got_ref[:, :HEAD]
    out_ref[:, :HEAD] = turn(keys, cos_ref[...], sin_ref[...]).astype(BF)
    values = own_ref[:, HEAD:] + got_ref[:, HEAD:]
    out_ref[:, HEAD:] = (values + lift_ref[...]).astype(BF)


def finish_keys(own, got, lift, cosine, sine):
    return call(
        keys_kernel,
        ROWS * 128 * 8,
        ROWS * 128 * 32,
        out_shape=jax.ShapeDtypeStruct((ROWS, 256), BF),
        in_specs=[pl.BlockSpec(memory_space=pltpu.VMEM)] * 5,
        out_specs=pl.BlockSpec(memory_space=pltpu.VMEM),
    )(own, got, lift, cosine, sine)


def against(queries, keys):
    return lax.dot_general(queries, keys, (((1,), (1,)), ((), ())), preferred_element_type=F32)


def attend(queries, first, pair_ref, anchor_ref):
    to_anchor = against(queries, anchor_ref[:, :HEAD])
    to_anchor = jnp.where(first, masked, to_anchor)
    to_own = against(queries, pair_ref[:, :HEAD])
    row = lax.broadcasted_iota(jnp.int32, (ROWS, ROWS), 0)
    col = lax.broadcasted_iota(jnp.int32, (ROWS, ROWS), 1)
    to_own = jnp.where(row >= col, to_own, masked)
    highest = jnp.maximum(
        jnp.max(to_anchor, axis=1, keepdims=True), jnp.max(to_own, axis=1, keepdims=True)
    )
    to_anchor = jnp.exp2((to_anchor - highest) * power)
    to_own = jnp.exp2((to_own - highest) * power)
    total = jnp.sum(to_anchor, axis=1, keepdims=True) + jnp.sum(to_own, axis=1, keepdims=True)
    share = 1.0 / total
    mixed = jnp.dot((to_anchor * share).astype(BF), anchor_ref[:, HEAD:], preferred_element_type=F32)
    return mixed + jnp.dot((to_own * share).astype(BF), pair_ref[:, HEAD:], preferred_element_type=F32)


def unpacked(group_ref):
    return jnp.concatenate([group_ref[:, g * HEAD : (g + 1) * HEAD] for g in range(7)], axis=0)


def context_kernel(
    number_ref, own_ref, got_ref, lift_ref, cos_ref, sin_ref, pair_ref, mine_ref, theirs_ref, out_ref, anchor_ref
):
    @pl.when(pl.program_id(0) == 0)
    def _():
        mine, theirs = unpacked(mine_ref), unpacked(theirs_ref)
        anchor_ref[:, :HEAD] = jnp.where(number_ref[CORE_AT] == 0, mine, theirs)
        anchor_ref[:, HEAD:] = jnp.where(number_ref[CORE_AT] == 0, theirs, mine)

    queries = own_ref[...] + got_ref[...] + lift_ref[...]
    for head in range(2):
        cols = slice(head * HEAD, (head + 1) * HEAD)
        turned = turn(queries[:, cols], cos_ref[...], sin_ref[...]).astype(BF)
        out_ref[:, cols] = attend(turned, number_ref[BLOCK_ID] == 0, pair_ref, anchor_ref).astype(BF)


def context_attention(numbers, own, got, lift, cosine, sine, pair, mine, theirs):
    wide = pl.BlockSpec((ROWS, 256), lambda i: (0, 0))
    thin = pl.BlockSpec((ROWS, 128), lambda i: (0, 0))
    heads = pl.BlockSpec((ROWS, 256), lambda i: (0, i))
    packed = pl.BlockSpec((64, 1152), lambda i: (0, 0))
    return call(
        context_kernel,
        64 * ROWS * ROWS * HEAD,
        ROWS * 1024 * 14,
        16 * ROWS * ROWS,
        out_shape=jax.ShapeDtypeStruct((ROWS, 1024), BF),
        grid=(4,),
        in_specs=[pl.BlockSpec(memory_space=pltpu.SMEM), heads, heads, heads, thin, thin, wide, packed, packed],
        out_specs=heads,
        scratch_shapes=[pltpu.VMEM((ROWS, 256), BF)],
    )(numbers, own, got, lift, cosine, sine, pair, mine, theirs)


def pack_stats(stats):
    high = stats.astype(BF).astype(F32)
    rest = stats - high
    middle = rest.astype(BF).astype(F32)
    low = rest - middle
    return high + pltpu.roll(middle, 16, 1) + pltpu.roll(low, 32, 1)


def unpack_stats(group):
    terms = group.astype(F32)
    return terms + pltpu.roll(terms, 112, 1) + pltpu.roll(terms, 96, 1)


def stats_of(maxima, totals):
    rows = maxima[0].shape[0]
    lane = lax.broadcasted_iota(jnp.int32, (rows, 128), 1)
    stats = jnp.zeros((rows, 128), F32)
    for at, column in enumerate(maxima + totals):
        stats = jnp.where(lane == at, column, stats)
    return stats


def put(keep_ref, send_ref, top, cols, value, group, flag, stats=False):
    half = value.shape[0] // 2
    split = value.reshape(half // group, 2, group, value.shape[1])
    low, high = split[:, 0].reshape(half, -1), split[:, 1].reshape(half, -1)
    keep_ref[:, cols] = jnp.where(flag, high, low)
    sent = jnp.where(flag, low, high)
    if stats:
        sent = pack_stats(sent)
    if half < 16:
        sent = jnp.concatenate([sent, sent], axis=0)
    send_ref[top:, cols] = sent.astype(BF)


def query_kernel(number_ref, lines_ref, pair_ref, keep_ref, send_ref, query_ref):
    for side in range(2):
        for at_x in range(XS):
            back = lax.rem(number_ref[PLACE_X] + XS - at_x, XS)
            for pair in range(4):
                rows = []
                for place in (2 * pair, 2 * pair + 1):
                    block = lines_ref[back, place, 128 + 32 * side : 160 + 32 * side].astype(F32)
                    rows.append(jnp.concatenate([block[8 * g : 8 * g + 8] for g in range(4)], axis=1))
                at = 256 * side + 64 * at_x + 16 * pair
                query_ref[at : at + 16] = jnp.concatenate(rows, axis=0).astype(BF)

    send_ref[:128, 896:] = jnp.zeros((128, 256), BF)
    for half in range(2):
        cols = slice(half * HEAD, (half + 1) * HEAD)
        for g in range(7):
            piece = pair_ref[g * 64 : g * 64 + 64, cols]
            send_ref[half * 64 : half * 64 + 64, g * HEAD : (g + 1) * HEAD] = jnp.where(
                number_ref[BLOCK_ID] == 0, piece, jnp.zeros_like(piece)
            )
    rows = query_ref.shape[0]
    maxima, totals = [], []
    for head in range(8):
        cols = slice(head * HEAD, (head + 1) * HEAD)
        scores = against(query_ref[:, cols], pair_ref[:, :HEAD])
        highest = jnp.max(scores, axis=1, keepdims=True)
        weights = jnp.exp2((scores - highest) * power)
        maxima.append(highest * scale)
        totals.append(jnp.sum(weights, axis=1, keepdims=True))
        sums = jnp.dot(weights.astype(BF), pair_ref[:, HEAD:], preferred_element_type=F32)
        put(keep_ref, send_ref, 128, cols, sums, rows // 2, False)
    put(keep_ref, send_ref, 128, slice(1024, 1152), stats_of(maxima, totals), rows // 2, False, True)


def merge_kernel(group, at_flag, number_ref, mine_ref, sent_ref, got_ref, *out):
    flag = number_ref[at_flag] == 1
    rows = mine_ref.shape[0]
    top = 64 if rows < 256 else 128
    anchor = sent_ref[:top] + got_ref[:top]
    if top == 128:
        anchor = jnp.where(number_ref[CORE_AT] == 0, anchor[:64], anchor[64:])
    out[1][:64] = anchor
    lane = lax.broadcasted_iota(jnp.int32, (rows, 128), 1)
    one, two = mine_ref[:, 1024:], unpack_stats(got_ref[top:, 1024:])[:rows]
    highest = jnp.maximum(one, two)
    left = jnp.exp(jnp.where(lane < 8, one - highest, 0.0))
    right = jnp.exp(jnp.where(lane < 8, two - highest, 0.0))
    totals = one * pltpu.roll(left, 8, 1) + two * pltpu.roll(right, 8, 1)
    for head in range(8):
        cols = slice(head * HEAD, (head + 1) * HEAD)
        at = slice(head, head + 1)
        other = got_ref[top:, cols].astype(F32)[:rows]
        merged = mine_ref[:, cols] * left[:, at] + other * right[:, at]
        if group is None:
            out[0][:, cols] = (merged / totals[:, head + 8 : head + 9]).astype(BF)
        else:
            put(out[0], out[1], 64, cols, merged, group, flag)
    if group is not None:
        stats = jnp.where(lane < 8, highest, jnp.where(lane < 16, totals, 0.0))
        put(out[0], out[1], 64, slice(1024, 1152), stats, group, flag, True)


VMEM_BLOCK = pl.BlockSpec(memory_space=pltpu.VMEM)


def query_attention(numbers, lines, pair):
    rows = 512
    return call(
        query_kernel,
        32 * rows * ROWS * HEAD,
        rows * 1024 * 6,
        8 * rows * ROWS,
        out_shape=(
            jax.ShapeDtypeStruct((rows // 2, 1152), F32),
            jax.ShapeDtypeStruct((128 + rows // 2, 1152), BF),
        ),
        in_specs=[pl.BlockSpec(memory_space=pltpu.SMEM)] + [VMEM_BLOCK] * 2,
        out_specs=(VMEM_BLOCK,) * 2,
        scratch_shapes=[pltpu.VMEM((rows, 1024), BF)],
    )(numbers, lines, pair)


def merge(numbers, mine, sent, got, at_flag=0, group=None):
    rows = mine.shape[0]
    if group is None:
        shapes = (jax.ShapeDtypeStruct((rows, 1024), BF), jax.ShapeDtypeStruct((64, 1152), BF))
    else:
        half = rows // 2
        shapes = (
            jax.ShapeDtypeStruct((half, 1152), F32),
            jax.ShapeDtypeStruct((64 + max(half, 16), 1152), BF),
        )
    return call(
        functools.partial(merge_kernel, group, at_flag),
        8 * rows * 1024,
        rows * 1152 * 8,
        out_shape=shapes,
        in_specs=[pl.BlockSpec(memory_space=pltpu.SMEM)] + [VMEM_BLOCK] * 3,
        out_specs=(VMEM_BLOCK,) * 2,
    )(numbers, mine, sent, got)


def tie(*values):
    return lax.optimization_barrier(values)


def doubled(piece, bit_set, got):
    return jnp.concatenate([jnp.where(bit_set, got, piece), jnp.where(bit_set, piece, got)], axis=0)


def shards(
    hidden,
    query_rows,
    query_weight,
    key_weight,
    value_weight,
    query_down,
    value_down,
    query_up,
    value_up,
    block_order,
    tenant,
):
    my_index = lax.axis_index("ctx")
    x, z, core = my_index // 16, lax.rem(my_index // 2, ZS), lax.rem(my_index, 2)
    y = lax.axis_index("tp")
    block_id = lax.dynamic_index_in_dim(block_order, my_index, 0, keepdims=False)
    owner = lax.dynamic_index_in_dim(tenant, block_id, 0, keepdims=False)
    flags = [x % 2, x // 2, z % 2, (z // 2) % 2, z // 4]
    around = lax.rem(x - y + XS, XS)
    numbers = jnp.stack([around, block_id, core, x, owner] + flags).astype(jnp.int32)
    fx, bx = (lambda v: ctx_move(v, dx=1)), (lambda v: ctx_move(v, dx=-1))
    fz, bz = (lambda v: ctx_move(v, dz=1)), (lambda v: ctx_move(v, dz=-1))

    packed = query_rows.reshape(8, 4, 256).transpose(1, 0, 2).reshape(32, 256)
    blank = jnp.zeros((LINE_SENT - LINE, 256), BF)
    line = jnp.concatenate(
        [jnp.concatenate([key_weight, value_weight], axis=1), packed, swap_core(packed), blank], axis=0
    )
    line = gather_z(line[None])
    own, theirs = split_parity(core, hidden)
    own_1 = move_y(own, 1)
    other = swap_core(theirs)
    other_1 = move_y(other, -1)
    weight = jnp.stack([query_weight, fx(query_weight), ctx_move(query_weight, dx=2), bx(query_weight)])
    own_1, other_1, weight, hidden = tie(own_1, other_1, weight, hidden)
    own_2, other_2 = move_y(own_1, 1), move_y(other_1, -1)
    low = low_parts(numbers, hidden, query_down, value_down)
    own_2, other_2, line, weight, low = tie(own_2, other_2, line, weight, low)
    weight = gather_z(weight[None])
    line = line[:, :LINE]
    ahead, behind = fx(line), bx(line)
    own_3, other_3 = move_y(own_2, 1), move_y(other_2, -1)
    low = low + lax.ppermute(low, "tp", [(i, i ^ 1) for i in range(YS)])
    own_3, other_3, ahead, behind, low = tie(own_3, other_3, ahead, behind, low)
    far = jnp.concatenate([fx(ahead[:4]), bx(behind[4:])], axis=0)
    low = low + lax.ppermute(low, "tp", [(i, i ^ 2) for i in range(YS)])
    lines = jnp.stack([line, ahead, far, behind])
    own_tokens = (own, own_1, own_2, own_3)
    other_tokens = (other, other_1, other_2, other_3)

    low = low.astype(BF)
    over_rank = (((0,), (0,)), ((), ()))
    query_lift = lax.dot_general(
        low[:RANK], lax.dynamic_index_in_dim(query_up, owner, 0, keepdims=False), over_rank, preferred_element_type=F32
    )
    value_lift = lax.dot_general(
        low[RANK:], lax.dynamic_index_in_dim(value_up, owner, 0, keepdims=False), over_rank, preferred_element_type=F32
    )
    half = HEAD // 2
    positions = block_id * ROWS + jnp.arange(ROWS, dtype=jnp.int32)
    frequency = rope_base ** (-(jnp.arange(half, dtype=F32) / half))
    angles = positions.astype(F32)[:, None] * frequency[None, :]
    cosine, sine = jnp.cos(angles), jnp.sin(angles)
    cosine = jnp.concatenate([cosine, cosine], axis=1)
    sine = jnp.concatenate([-sine, sine], axis=1)

    own_part, part = project(numbers, own_tokens, other_tokens, lines)
    pair = finish_keys(own_part, swap_core(part), value_lift, cosine, sine)

    keep, send = query_attention(numbers, lines, pair)
    for bit, at, group in ((CORE, 0, 64), (X1, 1, 64), (X2, 2, 8)):
        keep, send = merge(numbers, keep, send, ctx_flip(send, bit), FLAGS + at, group)
    got, parts = tie(ctx_flip(send, Z1), project(numbers, own_tokens, other_tokens, weight))
    own_part, part = parts
    keep, send = merge(numbers, keep, send, got, FLAGS + 3, 8)
    got, got_part = tie(ctx_flip(send, Z2), swap_core(part))
    keep, send = merge(numbers, keep, send, got, FLAGS + 4, 8)
    answer, mine = merge(numbers, keep, send, ctx_flip(send, Z4))
    context = context_attention(
        numbers, own_part, got_part, query_lift, cosine, sine, pair, mine, swap_core(mine)
    )
    return (context, answer)


def solution(mesh):
    placed = (
        P("ctx", "tp"),
        P("ctx", "tp"),
        P("ctx", "tp"),
        P("ctx", "tp"),
        P("ctx", "tp"),
        P("tp", None),
        P("tp", None),
        P(None, None, "tp"),
        P(None, None, "tp"),
        P(),
        P(),
    )
    return jax.shard_map(
        shards,
        mesh=mesh,
        in_specs=placed,
        out_specs=(P("ctx", "tp"), P("ctx", "tp")),
        check_vma=False,
    )
```

profile of v0, /device:TPU:1, one launch (start us, length us, event | category | flops | bytes accessed | tf_op | source)
XLA Modules:
  0.0 218.3 jit_solution(13427200542893211537)
XLA Ops:
  9.1 3.3 %collective-permute-start.1 = (bf16[448,1024]{1,0:T(8,128)(2,1)S(1)}, bf16[448,1024]{1,0:T(8,128)(2,1)}, u32[]{:S(2)}, u32[]{:S(2)}) collective-permute-start(bf16[448,1024]{1,0:T(8,128)(2,1)S(1)} %get-tuple-element.42), channel_id=1, source_target_pairs={{0,4},{4,0},{8,12},{12,8},{16,20},{20,16},{24,28},{28,24},{32,36},... | collective-permute-start | bytes 2752520 | tf_op jit(solution)/shard_map/ppermute | solution.py:38
  21.0 5.0 %collective-permute-done.5 = bf16[128,1024]{1,0:T(8,128)(2,1)S(1)} collective-permute-done((bf16[128,1024]{1,0:T(8,128)(2,1)}, bf16[128,1024]{1,0:T(8,128)(2,1)S(1)}, u32[]{:S(2)}, u32[]{:S(2)}) %collective-permute-start.5) | collective-permute-done | bytes 262176 | tf_op jit(solution)/shard_map/ppermute | solution.py:38
  28.5 7.0 %collective-permute-done.3 = bf16[128,1024]{1,0:T(8,128)(2,1)S(1)} collective-permute-done((bf16[128,1024]{1,0:T(8,128)(2,1)}, bf16[128,1024]{1,0:T(8,128)(2,1)S(1)}, u32[]{:S(2)}, u32[]{:S(2)}) %collective-permute-start.3) | collective-permute-done | bytes 262176 | tf_op jit(solution)/shard_map/ppermute | solution.py:38
  37.7 2.7 %collective-permute-start.7 = (bf16[448,1024]{1,0:T(8,128)(2,1)}, bf16[448,1024]{1,0:T(8,128)(2,1)}, u32[]{:S(2)}, u32[]{:S(2)}) collective-permute-start(bf16[448,1024]{1,0:T(8,128)(2,1)} %collective-permute-done.2.refs_5_), channel_id=1, source_target_pairs={{0,3},{1,0},{2,1},{3,2},{4,7},{5,4},{6,5},{7,6},{8,11},{9,8},{10,9... | collective-permute-start | bytes 2752520 | tf_op jit(solution)/shard_map/ppermute | solution.py:55
  48.6 3.6 %all-gather.5.cloned.1.call-done = bf16[2048,256]{1,0:T(8,128)(2,1)} async-done(((bf16[256,256]{1,0:T(8,128)(2,1)}), bf16[2048,256]{1,0:T(8,128)(2,1)}) %all-gather.5.cloned.1.call-update) | async-done | bytes 1048592 | tf_op jit(solution)/shard_map/all_gather | solution.py:51
  52.3 8.4 %collective-permute-done.6.refs_2_ = bf16[448,1024]{1,0:T(8,128)(2,1)} collective-permute-done((bf16[448,1024]{1,0:T(8,128)(2,1)}, bf16[448,1024]{1,0:T(8,128)(2,1)}, u32[]{:S(2)}, u32[]{:S(2)}) %collective-permute-start.6) | collective-permute-done | bytes 917536 | tf_op jit(solution)/shard_map/ppermute | solution.py:55
  60.8 2.7 %collective-permute-start.10 = (bf16[448,1024]{1,0:T(8,128)(2,1)}, bf16[448,1024]{1,0:T(8,128)(2,1)S(1)}, u32[]{:S(2)}, u32[]{:S(2)}) collective-permute-start(bf16[448,1024]{1,0:T(8,128)(2,1)} %collective-permute-done.7.refs_6_), channel_id=1, source_target_pairs={{0,3},{1,0},{2,1},{3,2},{4,7},{5,4},{6,5},{7,6},{8,11},{9,8},{10,9... | collective-permute-start | bytes 2752520 | tf_op jit(solution)/shard_map/ppermute | solution.py:55
  66.0 2.7 %collective-permute-start.12 = (bf16[8,192,256]{2,1,0:T(8,128)(2,1)}, bf16[8,192,256]{2,1,0:T(8,128)(2,1)}, u32[]{:S(2)}, u32[]{:S(2)}) collective-permute-start(bf16[8,192,256]{2,1,0:T(8,128)(2,1)} %get-tuple-element.81), channel_id=1, source_target_pairs={{0,192},{4,196},{8,200},{12,204},{16,208},{20,212},{24,216},{28,22... | collective-permute-start | bytes 2359304 | tf_op jit(solution)/shard_map/ppermute | solution.py:38
  69.5 13.8 %collective-permute-done.13 = f32[32,448]{1,0:T(8,128)S(1)} collective-permute-done((f32[32,448]{1,0:T(8,128)S(1)}, f32[32,448]{1,0:T(8,128)S(1)}, u32[]{:S(2)}, u32[]{:S(2)}) %collective-permute-start.13) | collective-permute-done | bytes 57376 | tf_op jit(solution)/shard_map/ppermute | solution.py:444
  86.1 2.7 %collective-permute-start.15 = (bf16[4,192,256]{2,1,0:T(8,128)(2,1)S(1)}, bf16[4,192,256]{2,1,0:T(8,128)(2,1)S(1)}, u32[]{:S(2)}, u32[]{:S(2)}) collective-permute-start(bf16[4,192,256]{2,1,0:T(8,128)(2,1)S(1)} %slice.17), channel_id=1, source_target_pairs={{0,192},{4,196},{8,200},{12,204},{16,208},{20,212},{24,216},{28,22... | collective-permute-start | bytes 1179656 | tf_op jit(solution)/shard_map/ppermute | solution.py:38
  91.6 2.9 %collective-permute-done.15 = bf16[4,192,256]{2,1,0:T(8,128)(2,1)S(1)} collective-permute-done((bf16[4,192,256]{2,1,0:T(8,128)(2,1)S(1)}, bf16[4,192,256]{2,1,0:T(8,128)(2,1)S(1)}, u32[]{:S(2)}, u32[]{:S(2)}) %collective-permute-start.15) | collective-permute-done | bytes 393248 | tf_op jit(solution)/shard_map/ppermute | solution.py:38
  94.5 3.1 %collective-permute-done.14 = bf16[4,192,256]{2,1,0:T(8,128)(2,1)S(1)} collective-permute-done((bf16[4,192,256]{2,1,0:T(8,128)(2,1)S(1)}, bf16[4,192,256]{2,1,0:T(8,128)(2,1)S(1)}, u32[]{:S(2)}, u32[]{:S(2)}) %collective-permute-start.14) | collective-permute-done | bytes 393248 | tf_op jit(solution)/shard_map/ppermute | solution.py:38
  99.9 5.2 %shard_map.124 = (f32[448,256]{1,0:T(8,128)S(1)}, f32[448,256]{1,0:T(8,128)}) custom-call(s32[10]{0:T(128)S(1)} %stack.67.number_ref, bf16[448,1024]{1,0:T(8,128)(2,1)S(1)} %copy-done.8, bf16[448,1024]{1,0:T(8,128)(2,1)} %collective-permute-done.refs_1_, bf16[448,1024]{1,0:T(8,128)(2,1)} %collective-permute-done.6.refs_2_, bf16[448,1024]{1,0:T(8,128)(2,1)S(1)} %copy-done.11, ...), custom_call_target="tpu_custom_call" | custom-call | flops 1879048192 | bytes 10354688 | tf_op jit(solution)/shard_map/pallas_call | solution.py:164
  105.9 4.1 %collective-permute-start.16 = (f32[448,256]{1,0:T(8,128)}, f32[448,256]{1,0:T(8,128)}, u32[]{:S(2)}, u32[]{:S(2)}) collective-permute-start(f32[448,256]{1,0:T(8,128)} %get-tuple-element.56), channel_id=1, source_target_pairs={{0,4},{4,0},{8,12},{12,8},{16,20},{20,16},{24,28},{28,24},{32,36},... | collective-permute-start | bytes 1376264 | tf_op jit(solution)/shard_map/ppermute | solution.py:38
  117.6 3.8 %shard_map.126 = (f32[256,1152]{1,0:T(8,128)S(1)}, bf16[384,1152]{1,0:T(8,128)(2,1)S(1)}) custom-call(s32[10]{0:T(128)S(1)} %stack.67.number_ref, bf16[4,8,192,256]{3,2,1,0:T(8,128)(2,1)S(1)} %pad_maximum_fusion.refs_8_.lines_ref, bf16[448,256]{1,0:T(8,128)(2,1)S(1)} %shard_map.125.pair_ref), custom_call_target="tpu_custom_call" | custom-call | flops 939524096 | bytes 3145728 | tf_op jit(solution)/shard_map/pallas_call | solution.py:358
  125.4 11.7 %collective-permute-done.19.got_ref = bf16[192,1152]{1,0:T(8,128)(2,1)S(1)} collective-permute-done((bf16[192,1152]{1,0:T(8,128)(2,1)S(1)}, bf16[192,1152]{1,0:T(8,128)(2,1)S(1)}, u32[]{:S(2)}, u32[]{:S(2)}) %collective-permute-start.19) | collective-permute-done | bytes 442400 | tf_op jit(solution)/shard_map/ppermute | solution.py:42
  138.3 9.2 %collective-permute-done.20.got_ref = bf16[128,1152]{1,0:T(8,128)(2,1)S(1)} collective-permute-done((bf16[128,1152]{1,0:T(8,128)(2,1)S(1)}, bf16[128,1152]{1,0:T(8,128)(2,1)S(1)}, u32[]{:S(2)}, u32[]{:S(2)}) %collective-permute-start.20) | collective-permute-done | bytes 294944 | tf_op jit(solution)/shard_map/ppermute | solution.py:42
  150.3 6.8 %all-gather.7.cloned.1.call-done = bf16[32,128,1024]{2,1,0:T(8,128)(2,1)} async-done(((bf16[4,128,1024]{2,1,0:T(8,128)(2,1)}), bf16[32,128,1024]{2,1,0:T(8,128)(2,1)}) %all-gather.7.cloned.1.call-update) | async-done | bytes 8388624 | tf_op jit(solution)/shard_map/all_gather | solution.py:51
  157.1 3.4 %copy-done.26 = bf16[32,128,1024]{2,1,0:T(8,128)(2,1)S(1)} copy-done((bf16[32,128,1024]{2,1,0:T(8,128)(2,1)S(1)}, bf16[32,128,1024]{2,1,0:T(8,128)(2,1)}, u32[]{:S(2)}) %copy-start.26) | copy-done | bytes 8388632
  160.5 10.1 %shard_map.130 = (f32[448,1024]{1,0:T(8,128)S(1)}, f32[448,1024]{1,0:T(8,128)S(1)}) custom-call(s32[10]{0:T(128)S(1)} %stack.67.number_ref, bf16[448,1024]{1,0:T(8,128)(2,1)S(1)} %copy-done.9, bf16[448,1024]{1,0:T(8,128)(2,1)} %collective-permute-done.refs_1_, bf16[448,1024]{1,0:T(8,128)(2,1)} %collective-permute-done.6.refs_2_, ...), custom_call_target="tpu_custom_call" | custom-call | flops 7516192768 | bytes 19398656 | tf_op jit(solution)/shard_map/pallas_call | solution.py:164
  174.3 9.5 %collective-permute-done.22.got_ref = bf16[80,1152]{1,0:T(8,128)(2,1)S(1)} collective-permute-done((bf16[80,1152]{1,0:T(8,128)(2,1)S(1)}, bf16[80,1152]{1,0:T(8,128)(2,1)S(1)}, u32[]{:S(2)}, u32[]{:S(2)}) %collective-permute-start.22) | collective-permute-done | bytes 184352 | tf_op jit(solution)/shard_map/ppermute | solution.py:42
  184.5 2.8 %collective-permute-start.24 = (bf16[80,1152]{1,0:T(8,128)(2,1)S(1)}, bf16[80,1152]{1,0:T(8,128)(2,1)S(1)}, u32[]{:S(2)}, u32[]{:S(2)}) collective-permute-start(bf16[80,1152]{1,0:T(8,128)(2,1)S(1)} %get-tuple-element.77.sent_ref), channel_id=1, source_target_pairs={{0,32},{4,36},{8,40},{12,44},{16,48},{20,52},{24,56},{28,60},{32,0... | collective-permute-start | bytes 552968 | tf_op jit(solution)/shard_map/ppermute | solution.py:42
  187.4 11.3 %collective-permute-done.24.got_ref = bf16[80,1152]{1,0:T(8,128)(2,1)S(1)} collective-permute-done((bf16[80,1152]{1,0:T(8,128)(2,1)S(1)}, bf16[80,1152]{1,0:T(8,128)(2,1)S(1)}, u32[]{:S(2)}, u32[]{:S(2)}) %collective-permute-start.24) | collective-permute-done | bytes 184352 | tf_op jit(solution)/shard_map/ppermute | solution.py:42
  201.6 9.9 %shard_map.134 = bf16[448,1024]{1,0:T(8,128)(2,1)} custom-call(s32[10]{0:T(128)S(1)} %stack.67.number_ref, f32[448,1024]{1,0:T(8,128)S(1)} %get-tuple-element.68.own_ref, f32[448,1024]{1,0:T(8,128)S(1)} %collective-permute-done.23.got_ref, f32[448,1024]{1,0:T(8,128)S(1)} %fusion.1.lift_ref, f32[448,128]{1,0:T(8,128)S(1)} %copy-done.4, ...), custom_call_target="tpu_custom_call" | custom-call | flops 1644167168 | bytes 6422528 | tf_op jit(solution)/shard_map/pallas_call | solution.py:243
  (129 shorter events, 53.6 us)
Async XLA Ops:
  7.2 45.1 %all-gather.5.cloned.1.call-start = ((), (), s32[]{:S(2)}) async-start(), calls=%async_computation | async-start | bytes 1179648 | tf_op jit(solution)/shard_map/all_gather | solution.py:51
  12.6 25.1 %collective-permute-start = (bf16[448,1024]{1,0:T(8,128)(2,1)S(1)}, bf16[448,1024]{1,0:T(8,128)(2,1)}, u32[]{:S(2)}, u32[]{:S(2)}) collective-permute-start(bf16[448,1024]{1,0:T(8,128)(2,1)S(1)} %get-tuple-element.41.refs_0_), channel_id=1, source_target_pairs={{0,1},{1,2},{2,3},{3,0},{4,5},{5,6},{6,7},{7,4},{8,9},{9,10},{10,1... | collective-permute-start | bytes 2752520 | tf_op jit(solution)/shard_map/ppermute | solution.py:55
  14.7 22.9 %collective-permute-start.2 = (bf16[448,1024]{1,0:T(8,128)(2,1)}, bf16[448,1024]{1,0:T(8,128)(2,1)}, u32[]{:S(2)}, u32[]{:S(2)}) collective-permute-start(bf16[448,1024]{1,0:T(8,128)(2,1)} %collective-permute-done.1.refs_4_), channel_id=1, source_target_pairs={{0,3},{1,0},{2,1},{3,2},{4,7},{5,4},{6,5},{7,6},{8,11},{9,8},{10,9... | collective-permute-start | bytes 2752520 | tf_op jit(solution)/shard_map/ppermute | solution.py:55
  17.3 139.8 %all-gather.7.cloned.1.call-start = ((), (), s32[]{:S(2)}) async-start(), calls=%async_computation.1 | async-start | bytes 9437184 | tf_op jit(solution)/shard_map/all_gather | solution.py:51
  17.3 8.7 %collective-permute-start.5 = (bf16[128,1024]{1,0:T(8,128)(2,1)}, bf16[128,1024]{1,0:T(8,128)(2,1)S(1)}, u32[]{:S(2)}, u32[]{:S(2)}) collective-permute-start(bf16[128,1024]{1,0:T(8,128)(2,1)} %param.13), channel_id=1, source_target_pairs={{0,192},{4,196},{8,200},{12,204},{16,208},{20,212},{24,216},{28,22... | collective-permute-start | bytes 786440 | tf_op jit(solution)/shard_map/ppermute | solution.py:38
  19.9 8.6 %collective-permute-start.4 = (bf16[128,1024]{1,0:T(8,128)(2,1)}, bf16[128,1024]{1,0:T(8,128)(2,1)S(1)}, u32[]{:S(2)}, u32[]{:S(2)}) collective-permute-start(bf16[128,1024]{1,0:T(8,128)(2,1)} %param.13), channel_id=1, source_target_pairs={{0,128},{4,132},{8,136},{12,140},{16,144},{20,148},{24,152},{28,15... | collective-permute-start | bytes 786440 | tf_op jit(solution)/shard_map/ppermute | solution.py:38
  20.4 15.1 %collective-permute-start.3 = (bf16[128,1024]{1,0:T(8,128)(2,1)}, bf16[128,1024]{1,0:T(8,128)(2,1)S(1)}, u32[]{:S(2)}, u32[]{:S(2)}) collective-permute-start(bf16[128,1024]{1,0:T(8,128)(2,1)} %param.13), channel_id=1, source_target_pairs={{0,64},{4,68},{8,72},{12,76},{16,80},{20,84},{24,88},{28,92},{32,9... | collective-permute-start | bytes 786440 | tf_op jit(solution)/shard_map/ppermute | solution.py:38
  37.6 23.1 %collective-permute-start.6 = (bf16[448,1024]{1,0:T(8,128)(2,1)}, bf16[448,1024]{1,0:T(8,128)(2,1)}, u32[]{:S(2)}, u32[]{:S(2)}) collective-permute-start(bf16[448,1024]{1,0:T(8,128)(2,1)} %collective-permute-done.refs_1_), channel_id=1, source_target_pairs={{0,1},{1,2},{2,3},{3,0},{4,5},{5,6},{6,7},{7,4},{8,9},{9,10},{10,1... | collective-permute-start | bytes 2752520 | tf_op jit(solution)/shard_map/ppermute | solution.py:55
  37.7 23.1 %collective-permute-start.7 = (bf16[448,1024]{1,0:T(8,128)(2,1)}, bf16[448,1024]{1,0:T(8,128)(2,1)}, u32[]{:S(2)}, u32[]{:S(2)}) collective-permute-start(bf16[448,1024]{1,0:T(8,128)(2,1)} %collective-permute-done.2.refs_5_), channel_id=1, source_target_pairs={{0,3},{1,0},{2,1},{3,2},{4,7},{5,4},{6,5},{7,6},{8,11},{9,8},{10,9... | collective-permute-start | bytes 2752520 | tf_op jit(solution)/shard_map/ppermute | solution.py:55
  60.8 24.0 %collective-permute-start.9 = (bf16[448,1024]{1,0:T(8,128)(2,1)}, bf16[448,1024]{1,0:T(8,128)(2,1)S(1)}, u32[]{:S(2)}, u32[]{:S(2)}) collective-permute-start(bf16[448,1024]{1,0:T(8,128)(2,1)} %collective-permute-done.6.refs_2_), channel_id=1, source_target_pairs={{0,1},{1,2},{2,3},{3,0},{4,5},{5,6},{6,7},{7,4},{8,9},{9,10},{10,1... | collective-permute-start | bytes 2752520 | tf_op jit(solution)/shard_map/ppermute | solution.py:55
  60.8 23.9 %collective-permute-start.10 = (bf16[448,1024]{1,0:T(8,128)(2,1)}, bf16[448,1024]{1,0:T(8,128)(2,1)S(1)}, u32[]{:S(2)}, u32[]{:S(2)}) collective-permute-start(bf16[448,1024]{1,0:T(8,128)(2,1)} %collective-permute-done.7.refs_6_), channel_id=1, source_target_pairs={{0,3},{1,0},{2,1},{3,2},{4,7},{5,4},{6,5},{7,6},{8,11},{9,8},{10,9... | collective-permute-start | bytes 2752520 | tf_op jit(solution)/shard_map/ppermute | solution.py:55
  65.9 18.8 %collective-permute-start.11 = (bf16[8,192,256]{2,1,0:T(8,128)(2,1)}, bf16[8,192,256]{2,1,0:T(8,128)(2,1)S(1)}, u32[]{:S(2)}, u32[]{:S(2)}) collective-permute-start(bf16[8,192,256]{2,1,0:T(8,128)(2,1)} %get-tuple-element.81), channel_id=1, source_target_pairs={{0,64},{4,68},{8,72},{12,76},{16,80},{20,84},{24,88},{28,92},{32,9... | collective-permute-start | bytes 2359304 | tf_op jit(solution)/shard_map/ppermute | solution.py:38
  66.0 18.8 %collective-permute-start.12 = (bf16[8,192,256]{2,1,0:T(8,128)(2,1)}, bf16[8,192,256]{2,1,0:T(8,128)(2,1)}, u32[]{:S(2)}, u32[]{:S(2)}) collective-permute-start(bf16[8,192,256]{2,1,0:T(8,128)(2,1)} %get-tuple-element.81), channel_id=1, source_target_pairs={{0,192},{4,196},{8,200},{12,204},{16,208},{20,212},{24,216},{28,22... | collective-permute-start | bytes 2359304 | tf_op jit(solution)/shard_map/ppermute | solution.py:38
  69.3 13.9 %collective-permute-start.13 = (f32[32,448]{1,0:T(8,128)S(1)}, f32[32,448]{1,0:T(8,128)S(1)}, u32[]{:S(2)}, u32[]{:S(2)}) collective-permute-start(f32[32,448]{1,0:T(8,128)S(1)} %copy-done.23), channel_id=1, source_target_pairs={{0,1},{1,0},{2,3},{3,2},{4,5},{5,4},{6,7},{7,6},{8,9},{9,8},{10,11... | collective-permute-start | bytes 172040 | tf_op jit(solution)/shard_map/ppermute | solution.py:444
  86.1 8.4 %collective-permute-start.15 = (bf16[4,192,256]{2,1,0:T(8,128)(2,1)S(1)}, bf16[4,192,256]{2,1,0:T(8,128)(2,1)S(1)}, u32[]{:S(2)}, u32[]{:S(2)}) collective-permute-start(bf16[4,192,256]{2,1,0:T(8,128)(2,1)S(1)} %slice.17), channel_id=1, source_target_pairs={{0,192},{4,196},{8,200},{12,204},{16,208},{20,212},{24,216},{28,22... | collective-permute-start | bytes 1179656 | tf_op jit(solution)/shard_map/ppermute | solution.py:38
  88.8 8.7 %collective-permute-start.14 = (bf16[4,192,256]{2,1,0:T(8,128)(2,1)S(1)}, bf16[4,192,256]{2,1,0:T(8,128)(2,1)S(1)}, u32[]{:S(2)}, u32[]{:S(2)}) collective-permute-start(bf16[4,192,256]{2,1,0:T(8,128)(2,1)S(1)} %slice.16), channel_id=1, source_target_pairs={{0,64},{4,68},{8,72},{12,76},{16,80},{20,84},{24,88},{28,92},{32,9... | collective-permute-start | bytes 1179656 | tf_op jit(solution)/shard_map/ppermute | solution.py:38
  90.8 20.9 %collective-permute-start.17 = (f32[32,448]{1,0:T(8,128)S(1)}, f32[32,448]{1,0:T(8,128)}, u32[]{:S(2)}, u32[]{:S(2)}) collective-permute-start(f32[32,448]{1,0:T(8,128)S(1)} %add.53), channel_id=1, source_target_pairs={{0,2},{1,3},{2,0},{3,1},{4,6},{5,7},{6,4},{7,5},{8,10},{9,11},{10,... | collective-permute-start | bytes 172040 | tf_op jit(solution)/shard_map/ppermute | solution.py:447
  105.9 7.5 %collective-permute-start.16 = (f32[448,256]{1,0:T(8,128)}, f32[448,256]{1,0:T(8,128)}, u32[]{:S(2)}, u32[]{:S(2)}) collective-permute-start(f32[448,256]{1,0:T(8,128)} %get-tuple-element.56), channel_id=1, source_target_pairs={{0,4},{4,0},{8,12},{12,8},{16,20},{20,16},{24,28},{28,24},{32,36},... | collective-permute-start | bytes 1376264 | tf_op jit(solution)/shard_map/ppermute | solution.py:38
  125.3 11.8 %collective-permute-start.19 = (bf16[192,1152]{1,0:T(8,128)(2,1)S(1)}, bf16[192,1152]{1,0:T(8,128)(2,1)S(1)}, u32[]{:S(2)}, u32[]{:S(2)}) collective-permute-start(bf16[192,1152]{1,0:T(8,128)(2,1)S(1)} %get-tuple-element.61.sent_ref), channel_id=1, source_target_pairs={{0,64},{4,68},{8,72},{12,76},{16,80},{20,84},{24,88},{28,92},{32,9... | collective-permute-start | bytes 1327112 | tf_op jit(solution)/shard_map/ppermute | solution.py:42
  138.2 9.3 %collective-permute-start.20 = (bf16[128,1152]{1,0:T(8,128)(2,1)S(1)}, bf16[128,1152]{1,0:T(8,128)(2,1)S(1)}, u32[]{:S(2)}, u32[]{:S(2)}) collective-permute-start(bf16[128,1152]{1,0:T(8,128)(2,1)S(1)} %get-tuple-element.63.sent_ref), channel_id=1, source_target_pairs={{0,128},{4,132},{8,136},{12,140},{16,144},{20,148},{24,152},{28,15... | collective-permute-start | bytes 884744 | tf_op jit(solution)/shard_map/ppermute | solution.py:42
  149.0 21.6 %collective-permute-start.21 = (bf16[96,1152]{1,0:T(8,128)(2,1)S(1)}, bf16[96,1152]{1,0:T(8,128)(2,1)S(1)}, u32[]{:S(2)}, u32[]{:S(2)}) collective-permute-start(bf16[96,1152]{1,0:T(8,128)(2,1)S(1)} %get-tuple-element.64.sent_ref), channel_id=1, source_target_pairs={{0,8},{4,12},{8,0},{12,4},{16,24},{20,28},{24,16},{28,20},{32,40},... | collective-permute-start | bytes 663560 | tf_op jit(solution)/shard_map/ppermute | solution.py:42
  170.6 13.1 %collective-permute-start.23 = (f32[448,1024]{1,0:T(8,128)S(1)}, f32[448,1024]{1,0:T(8,128)S(1)}, u32[]{:S(2)}, u32[]{:S(2)}) collective-permute-start(f32[448,1024]{1,0:T(8,128)S(1)} %get-tuple-element.72), channel_id=1, source_target_pairs={{0,4},{4,0},{8,12},{12,8},{16,20},{20,16},{24,28},{28,24},{32,36},... | collective-permute-start | bytes 5505032 | tf_op jit(solution)/shard_map/ppermute | solution.py:38
  172.6 11.1 %collective-permute-start.22 = (bf16[80,1152]{1,0:T(8,128)(2,1)S(1)}, bf16[80,1152]{1,0:T(8,128)(2,1)S(1)}, u32[]{:S(2)}, u32[]{:S(2)}) collective-permute-start(bf16[80,1152]{1,0:T(8,128)(2,1)S(1)} %get-tuple-element.71.sent_ref), channel_id=1, source_target_pairs={{0,16},{4,20},{8,24},{12,28},{16,0},{20,4},{24,8},{28,12},{32,48},... | collective-permute-start | bytes 552968 | tf_op jit(solution)/shard_map/ppermute | solution.py:42
  184.5 14.2 %collective-permute-start.24 = (bf16[80,1152]{1,0:T(8,128)(2,1)S(1)}, bf16[80,1152]{1,0:T(8,128)(2,1)S(1)}, u32[]{:S(2)}, u32[]{:S(2)}) collective-permute-start(bf16[80,1152]{1,0:T(8,128)(2,1)S(1)} %get-tuple-element.77.sent_ref), channel_id=1, source_target_pairs={{0,32},{4,36},{8,40},{12,44},{16,48},{20,52},{24,56},{28,60},{32,0... | collective-permute-start | bytes 552968 | tf_op jit(solution)/shard_map/ppermute | solution.py:42
  (35 other events, 715.7 us)
Sparse Core Ops, SparseCore 0:
  17.4 34.7 all-gather.4
  60.9 96.1 all-gather.6
where the time goes:
time: 221 us; the launch traced here: 218 us
  waiting for transfers between devices  101 us (46%)
  Pallas kernels  38.6 us (17%)
  starting transfers between devices  31.7 us (14%)
  between operations  19.1 us (9%)
  local copies, waits for them, and re-layouts  17.9 us (8%)
  other arithmetic  8.19 us (4%)
    ppermute x6, waiting for transfers between devices, ctx_flip(): return lax.ppermute(value, 'ctx', [(i, i ^ bit) for i in range(64)])  44.1 us
    ppermute x12, waiting for transfers between devices, ctx_move(): return lax.ppermute(value, 'ctx', pairs)  24.6 us
    ppermute x12, starting transfers between devices, ctx_move(): return lax.ppermute(value, 'ctx', pairs)  18.3 us
    pallas_call x2, Pallas kernels, project(): call(project_kernel, 4 * ROWS * 4096 * cols, 2 * 4096 * (2 * ROWS + cols)...  15.3 us
    ppermute x1, waiting for transfers between devices, shards(): low = low + lax.ppermute(low, 'tp', [(i, i ^ 1) for i in range(YS)])  13.8 us
    unnamed x62, local copies, waits for them, and re-layouts  11.5 us
    all_gather x2, waiting for transfers between devices, gather_z(): lax.all_gather(value, 'ctx', axis_index_groups=lines, axis=0, tiled=True)  10.5 us
    pallas_call x1, Pallas kernels, context_attention(): call(context_kernel, 64 * ROWS * ROWS * HEAD, ROWS * 1024 * 14, 16 * ROWS...  9.93 us
  transfers between devices with their start and end apart: 28, of which 17 were waited for; matrix products, arithmetic and copies ran while one was open for 7% of the time, Pallas kernels for 12%

commit v1 on v0

--- a/solution.py
+++ b/solution.py
@@ -82,115 +82,116 @@
     return buffer
 
 
-def call(kernel, flops, moved, exps=0, **kw):
+def call(kernel, flops, moved, exps=0, vmem=VMEM, **kw):
     return pl.pallas_call(
         kernel,
-        compiler_params=pltpu.CompilerParams(vmem_limit_bytes=VMEM),
+        compiler_params=pltpu.CompilerParams(vmem_limit_bytes=vmem),
         cost_estimate=pl.CostEstimate(flops=flops, bytes_accessed=moved, transcendentals=exps),
         **kw,
     )
 
 
-def parity_kernel(core_ref, hidden_ref, mine_ref, theirs_ref):
-    first = core_ref[0] == 0
+def pack_terms(values, step):
+    high = values.astype(BF).astype(F32)
+    rest = values - high
+    middle = rest.astype(BF).astype(F32)
+    low = rest - middle
+    return high + pltpu.roll(middle, step, 1) + pltpu.roll(low, 2 * step, 1)
+
+
+def unpack_terms(group, step):
+    terms = group.astype(F32)
+    return terms + pltpu.roll(terms, 128 - step, 1) + pltpu.roll(terms, 128 - 2 * step, 1)
+
+
+def theirs_kernel(core_ref, hidden_ref, out_ref):
     for block in range(8):
         even = hidden_ref[:, block * 256 : block * 256 + 128]
         odd = hidden_ref[:, block * 256 + 128 : block * 256 + 256]
-        mine_ref[:, block * 128 : block * 128 + 128] = jnp.where(first, even, odd)
-        theirs_ref[:, block * 128 : block * 128 + 128] = jnp.where(first, odd, even)
-
-
-def split_parity(core, hidden):
-    shape = jax.ShapeDtypeStruct((ROWS, 1024), BF)
+        out_ref[:, block * 128 : block * 128 + 128] = jnp.where(core_ref[0] == 0, odd, even)
+
+
+def theirs_of(core, hidden):
+    vmem = pl.BlockSpec(memory_space=pltpu.VMEM)
     return call(
-        parity_kernel,
+        theirs_kernel,
         0,
-        4 * ROWS * 2048,
-        out_shape=(shape, shape),
-        in_specs=[pl.BlockSpec(memory_space=pltpu.SMEM), pl.BlockSpec(memory_space=pltpu.VMEM)],
-        out_specs=(pl.BlockSpec(memory_space=pltpu.VMEM),) * 2,
+        3 * ROWS * 2048,
+        out_shape=jax.ShapeDtypeStruct((ROWS, 1024), BF),
+        in_specs=[pl.BlockSpec(memory_space=pltpu.SMEM), vmem],
+        out_specs=vmem,
     )(core.reshape(1), hidden)
 
 
-def low_kernel(number_ref, hidden_ref, query_ref, value_ref, out_ref):
+def own_kernel(number_ref, hidden_ref, query_ref, value_ref, out_ref):
     shift = number_ref[OWNER] * RANK
     low_q = jnp.dot(hidden_ref[...], query_ref[...], preferred_element_type=F32)
     low_v = jnp.dot(hidden_ref[...], value_ref[...], preferred_element_type=F32)
     low_q = pltpu.roll(low_q, lax.rem(128 - shift, 128), 1)
     low_v = pltpu.roll(low_v, lax.rem(128 + RANK - shift, 128), 1)
     lane = lax.broadcasted_iota(jnp.int32, low_q.shape, 1)
-    out_ref[...] = jnp.where(lane < RANK, low_q, low_v).T[: 2 * RANK]
-
-
-def low_parts(numbers, hidden, query_down, value_down):
+    low = jnp.where(lane < RANK, low_q, jnp.where(lane < 2 * RANK, low_v, 0.0))
+    out_ref[:, 1024:] = pack_terms(low, 2 * RANK).astype(BF)
+    first = number_ref[CORE_AT] == 0
+    for block in range(8):
+        even = hidden_ref[:, block * 256 : block * 256 + 128]
+        odd = hidden_ref[:, block * 256 + 128 : block * 256 + 256]
+        out_ref[:, block * 128 : block * 128 + 128] = jnp.where(first, even, odd)
+
+
+def own_of(numbers, hidden, query_down, value_down):
     vmem = pl.BlockSpec(memory_space=pltpu.VMEM)
     return call(
-        low_kernel,
+        own_kernel,
         2 * ROWS * 2048 * 256,
-        2 * 2048 * (ROWS + 256),
-        out_shape=jax.ShapeDtypeStruct((2 * RANK, ROWS), F32),
+        3 * ROWS * 2048 + 2 * 2048 * 256,
+        out_shape=jax.ShapeDtypeStruct((ROWS, 1152), BF),
         in_specs=[pl.BlockSpec(memory_space=pltpu.SMEM)] + [vmem] * 3,
         out_specs=vmem,
     )(numbers, hidden, query_down, value_down)
 
 
-def both(step, own_refs, other_refs):
-    return jnp.concatenate([own_refs[step][...], other_refs[(YS - step) % YS][...]], axis=0)
-
-
 def project_kernel(number_ref, *refs):
     own_refs, other_refs, weight_ref, own_out, other_out = refs[:4], refs[4:8], refs[8], refs[9], refs[10]
-    for tile in range(own_out.shape[1] // 256):
-        cols = slice(tile * 256, tile * 256 + 256)
-        sums = None
-        for step in range(YS):
-            at = lax.rem(number_ref[AROUND] + step, YS)
-            if weight_ref.shape[0] == XS:
-                blocks = [weight_ref[at, block, :128, cols] for block in range(ZS)]
-            else:
-                blocks = [weight_ref[block, at, :, cols] for block in range(ZS)]
-            product = jnp.dot(
-                both(step, own_refs, other_refs), jnp.concatenate(blocks, axis=0), preferred_element_type=F32
-            )
-            sums = product if sums is None else sums + product
-        own_out[:, cols] = sums[:ROWS]
-        other_out[:, cols] = sums[ROWS:]
-
-
-def project(numbers, own, other, weight):
-    cols = weight.shape[-1]
+    if len(refs) == 12:
+        low = sum(unpack_terms(ref[:, 1024:], 2 * RANK) for ref in own_refs)
+        lane = lax.broadcasted_iota(jnp.int32, low.shape, 1)
+        refs[11][...] = jnp.where(lane < 2 * RANK, low, 0.0).astype(BF)
+    sums = None
+    for step in range(YS):
+        at = lax.rem(number_ref[AROUND] + step, YS)
+        if weight_ref.shape[0] == XS:
+            blocks = [weight_ref[at, block, :128] for block in range(ZS)]
+        else:
+            blocks = [weight_ref[block, at] for block in range(ZS)]
+        tokens = jnp.concatenate([own_refs[step][:, :1024], other_refs[step][...]], axis=0)
+        product = jnp.dot(tokens, jnp.concatenate(blocks, axis=0), preferred_element_type=F32)
+        sums = product if sums is None else sums + product
+    own_out[...] = sums[:ROWS]
+    other_out[...] = sums[ROWS:]
+
+
+def project(numbers, tokens, weight, at=0, cols=256):
     out = jax.ShapeDtypeStruct((ROWS, cols), F32)
     vmem = pl.BlockSpec(memory_space=pltpu.VMEM)
+    tile = pl.BlockSpec((ROWS, 256), lambda i: (0, i))
+    window = None
+    if cols > 256:
+        window = pl.BlockSpec(weight.shape[:-1] + (256,), lambda i: (0, 0, 0, i + at))
     return call(
         project_kernel,
         4 * ROWS * 4096 * cols,
         2 * 4096 * (2 * ROWS + cols) + 8 * ROWS * cols,
-        out_shape=(out, out),
-        in_specs=[pl.BlockSpec(memory_space=pltpu.SMEM)] + [vmem] * 9,
-        out_specs=(vmem, vmem),
-    )(numbers, *own, *other, weight)
+        vmem=VMEM if cols == 256 else 50 * 1024 * 1024,
+        out_shape=(out, out) + ((jax.ShapeDtypeStruct((ROWS, 128), BF),) if cols == 256 else ()),
+        grid=(cols // 256,),
+        in_specs=[pl.BlockSpec(memory_space=pltpu.SMEM)] + [vmem] * 8 + [vmem if cols == 256 else window],
+        out_specs=(tile, tile) + ((pl.BlockSpec((ROWS, 128), lambda i: (0, 0)),) if cols == 256 else ()),
+    )(numbers, *tokens, weight)
 
 
 def turn(values, cosine, sine):
     return values * cosine + pltpu.roll(values, HEAD // 2, 1) * sine
-
-
-def keys_kernel(own_ref, got_ref, lift_ref, cos_ref, sin_ref, out_ref):
-    keys = own_ref[:, :HEAD] + got_ref[:, :HEAD]
-    out_ref[:, :HEAD] = turn(keys, cos_ref[...], sin_ref[...]).astype(BF)
-    values = own_ref[:, HEAD:] + got_ref[:, HEAD:]
-    out_ref[:, HEAD:] = (values + lift_ref[...]).astype(BF)
-
-
-def finish_keys(own, got, lift, cosine, sine):
-    return call(
-        keys_kernel,
-        ROWS * 128 * 8,
-        ROWS * 128 * 32,
-        out_shape=jax.ShapeDtypeStruct((ROWS, 256), BF),
-        in_specs=[pl.BlockSpec(memory_space=pltpu.VMEM)] * 5,
-        out_specs=pl.BlockSpec(memory_space=pltpu.VMEM),
-    )(own, got, lift, cosine, sine)
 
 
 def against(queries, keys):
@@ -220,25 +221,44 @@
 
 
 def context_kernel(
-    number_ref, own_ref, got_ref, lift_ref, cos_ref, sin_ref, pair_ref, mine_ref, theirs_ref, out_ref, anchor_ref
+    number_ref,
+    own_ref,
+    got_ref,
+    own_late_ref,
+    got_late_ref,
+    low_ref,
+    up_ref,
+    cos_ref,
+    sin_ref,
+    pair_ref,
+    mine_ref,
+    theirs_ref,
+    out_ref,
+    anchor_ref,
 ):
-    @pl.when(pl.program_id(0) == 0)
+    step = pl.program_id(0)
+
+    @pl.when(step == 0)
     def _():
         mine, theirs = unpacked(mine_ref), unpacked(theirs_ref)
         anchor_ref[:, :HEAD] = jnp.where(number_ref[CORE_AT] == 0, mine, theirs)
         anchor_ref[:, HEAD:] = jnp.where(number_ref[CORE_AT] == 0, theirs, mine)
 
-    queries = own_ref[...] + got_ref[...] + lift_ref[...]
+    queries = jnp.where(step < 2, own_ref[...] + got_ref[...], own_late_ref[...] + got_late_ref[...])
+    queries = queries + jnp.dot(low_ref[...], up_ref[...], preferred_element_type=F32)
     for head in range(2):
         cols = slice(head * HEAD, (head + 1) * HEAD)
         turned = turn(queries[:, cols], cos_ref[...], sin_ref[...]).astype(BF)
         out_ref[:, cols] = attend(turned, number_ref[BLOCK_ID] == 0, pair_ref, anchor_ref).astype(BF)
 
 
-def context_attention(numbers, own, got, lift, cosine, sine, pair, mine, theirs):
+def context_attention(numbers, early, late, low, up, cosine, sine, pair, mine, theirs):
     wide = pl.BlockSpec((ROWS, 256), lambda i: (0, 0))
     thin = pl.BlockSpec((ROWS, 128), lambda i: (0, 0))
     heads = pl.BlockSpec((ROWS, 256), lambda i: (0, i))
+    lifts = pl.BlockSpec((128, 256), lambda i: (0, i))
+    first = pl.BlockSpec((ROWS, 256), lambda i: (0, jnp.minimum(i, 1)))
+    last = pl.BlockSpec((ROWS, 256), lambda i: (0, jnp.maximum(i - 2, 0)))
     packed = pl.BlockSpec((64, 1152), lambda i: (0, 0))
     return call(
         context_kernel,
@@ -247,23 +267,11 @@
         16 * ROWS * ROWS,
         out_shape=jax.ShapeDtypeStruct((ROWS, 1024), BF),
         grid=(4,),
-        in_specs=[pl.BlockSpec(memory_space=pltpu.SMEM), heads, heads, heads, thin, thin, wide, packed, packed],
+        in_specs=[pl.BlockSpec(memory_space=pltpu.SMEM)]
+        + [first, first, last, last, thin, lifts, thin, thin, wide, packed, packed],
         out_specs=heads,
         scratch_shapes=[pltpu.VMEM((ROWS, 256), BF)],
-    )(numbers, own, got, lift, cosine, sine, pair, mine, theirs)
-
-
-def pack_stats(stats):
-    high = stats.astype(BF).astype(F32)
-    rest = stats - high
-    middle = rest.astype(BF).astype(F32)
-    low = rest - middle
-    return high + pltpu.roll(middle, 16, 1) + pltpu.roll(low, 32, 1)
-
-
-def unpack_stats(group):
-    terms = group.astype(F32)
-    return terms + pltpu.roll(terms, 112, 1) + pltpu.roll(terms, 96, 1)
+    )(numbers, *early, *late, low, up, cosine, sine, pair, mine, theirs)
 
 
 def stats_of(maxima, totals):
@@ -282,13 +290,31 @@
     keep_ref[:, cols] = jnp.where(flag, high, low)
     sent = jnp.where(flag, low, high)
     if stats:
-        sent = pack_stats(sent)
+        sent = pack_terms(sent, 16)
     if half < 16:
         sent = jnp.concatenate([sent, sent], axis=0)
     send_ref[top:, cols] = sent.astype(BF)
 
 
-def query_kernel(number_ref, lines_ref, pair_ref, keep_ref, send_ref, query_ref):
+def query_kernel(
+    number_ref,
+    lines_ref,
+    own_ref,
+    got_ref,
+    low_ref,
+    up_ref,
+    cos_ref,
+    sin_ref,
+    keep_ref,
+    send_ref,
+    pair_ref,
+    query_ref,
+):
+    lift = jnp.dot(low_ref[...], up_ref[...], preferred_element_type=F32)
+    keys = own_ref[:, :HEAD] + got_ref[:, :HEAD]
+    pair_ref[:, :HEAD] = turn(keys, cos_ref[...], sin_ref[...]).astype(BF)
+    pair_ref[:, HEAD:] = (own_ref[:, HEAD:] + got_ref[:, HEAD:] + lift).astype(BF)
+
     for side in range(2):
         for at_x in range(XS):
             back = lax.rem(number_ref[PLACE_X] + XS - at_x, XS)
@@ -331,7 +357,7 @@
         anchor = jnp.where(number_ref[CORE_AT] == 0, anchor[:64], anchor[64:])
     out[1][:64] = anchor
     lane = lax.broadcasted_iota(jnp.int32, (rows, 128), 1)
-    one, two = mine_ref[:, 1024:], unpack_stats(got_ref[top:, 1024:])[:rows]
+    one, two = mine_ref[:, 1024:], unpack_terms(got_ref[top:, 1024:], 16)[:rows]
     highest = jnp.maximum(one, two)
     left = jnp.exp(jnp.where(lane < 8, one - highest, 0.0))
     right = jnp.exp(jnp.where(lane < 8, two - highest, 0.0))
@@ -353,7 +379,7 @@
 VMEM_BLOCK = pl.BlockSpec(memory_space=pltpu.VMEM)
 
 
-def query_attention(numbers, lines, pair):
+def query_attention(numbers, lines, own, got, low, up, cosine, sine):
     rows = 512
     return call(
         query_kernel,
@@ -363,11 +389,12 @@
         out_shape=(
             jax.ShapeDtypeStruct((rows // 2, 1152), F32),
             jax.ShapeDtypeStruct((128 + rows // 2, 1152), BF),
+            jax.ShapeDtypeStruct((ROWS, 256), BF),
         ),
-        in_specs=[pl.BlockSpec(memory_space=pltpu.SMEM)] + [VMEM_BLOCK] * 2,
-        out_specs=(VMEM_BLOCK,) * 2,
+        in_specs=[pl.BlockSpec(memory_space=pltpu.SMEM)] + [VMEM_BLOCK] * 7,
+        out_specs=(VMEM_BLOCK,) * 3,
         scratch_shapes=[pltpu.VMEM((rows, 1024), BF)],
-    )(numbers, lines, pair)
+    )(numbers, lines, own, got, low, up, cosine, sine)
 
 
 def merge(numbers, mine, sent, got, at_flag=0, group=None):
@@ -428,35 +455,26 @@
         [jnp.concatenate([key_weight, value_weight], axis=1), packed, swap_core(packed), blank], axis=0
     )
     line = gather_z(line[None])
-    own, theirs = split_parity(core, hidden)
-    own_1 = move_y(own, 1)
-    other = swap_core(theirs)
-    other_1 = move_y(other, -1)
+    other = swap_core(theirs_of(core, hidden))
+    other_1, other_3 = move_y(other, 1), move_y(other, -1)
     weight = jnp.stack([query_weight, fx(query_weight), ctx_move(query_weight, dx=2), bx(query_weight)])
-    own_1, other_1, weight, hidden = tie(own_1, other_1, weight, hidden)
-    own_2, other_2 = move_y(own_1, 1), move_y(other_1, -1)
-    low = low_parts(numbers, hidden, query_down, value_down)
-    own_2, other_2, line, weight, low = tie(own_2, other_2, line, weight, low)
+    own = own_of(numbers, hidden, query_down, value_down)
+    other_1, other_3, weight, own = tie(other_1, other_3, weight, own)
+    own_1, own_3 = move_y(own, 1), move_y(own, -1)
+    line, weight = tie(line, weight)
     weight = gather_z(weight[None])
     line = line[:, :LINE]
     ahead, behind = fx(line), bx(line)
-    own_3, other_3 = move_y(own_2, 1), move_y(other_2, -1)
-    low = low + lax.ppermute(low, "tp", [(i, i ^ 1) for i in range(YS)])
-    own_3, other_3, ahead, behind, low = tie(own_3, other_3, ahead, behind, low)
-    far = jnp.concatenate([fx(ahead[:4]), bx(behind[4:])], axis=0)
-    low = low + lax.ppermute(low, "tp", [(i, i ^ 2) for i in range(YS)])
-    lines = jnp.stack([line, ahead, far, behind])
-    own_tokens = (own, own_1, own_2, own_3)
-    other_tokens = (other, other_1, other_2, other_3)
-
-    low = low.astype(BF)
-    over_rank = (((0,), (0,)), ((), ()))
-    query_lift = lax.dot_general(
-        low[:RANK], lax.dynamic_index_in_dim(query_up, owner, 0, keepdims=False), over_rank, preferred_element_type=F32
-    )
-    value_lift = lax.dot_general(
-        low[RANK:], lax.dynamic_index_in_dim(value_up, owner, 0, keepdims=False), over_rank, preferred_element_type=F32
-    )
+    own_1, own_3, other_3, ahead, behind = tie(own_1, own_3, other_3, ahead, behind)
+    own_2, other_2 = move_y(own_1, 1), move_y(other_3, -1)
+    far = (fx(ahead[:4]), bx(behind[4:]))
+
+    tokens = (own, own_1, own_2, own_3, other, other_1, other_2, other_3)
+
+    query_up = lax.dynamic_index_in_dim(query_up, owner, 0, keepdims=False)
+    value_up = lax.dynamic_index_in_dim(value_up, owner, 0, keepdims=False)
+    query_up = jnp.pad(query_up, ((0, 128 - RANK), (0, 0)))
+    value_up = jnp.pad(value_up, ((RANK, 128 - 2 * RANK), (0, 0)))
     half = HEAD // 2
     positions = block_id * ROWS + jnp.arange(ROWS, dtype=jnp.int32)
     frequency = rope_base ** (-(jnp.arange(half, dtype=F32) / half))
@@ -465,20 +483,30 @@
     cosine = jnp.concatenate([cosine, cosine], axis=1)
     sine = jnp.concatenate([-sine, sine], axis=1)
 
-    own_part, part = project(numbers, own_tokens, other_tokens, lines)
-    pair = finish_keys(own_part, swap_core(part), value_lift, cosine, sine)
-
-    keep, send = query_attention(numbers, lines, pair)
-    for bit, at, group in ((CORE, 0, 64), (X1, 1, 64), (X2, 2, 8)):
+    far, cosine, sine, value_up = tie(far, cosine, sine, value_up)
+    lines = jnp.stack([line, ahead, jnp.concatenate(far, axis=0), behind])
+    own_part, part, low = project(numbers, tokens, lines)
+    keep, send, pair = query_attention(numbers, lines, own_part, swap_core(part), low, value_up, cosine, sine)
+    for bit, at, group in ((CORE, 0, 64), (X1, 1, 64), (X2, 2, 8), (Z1, 3, 8)):
         keep, send = merge(numbers, keep, send, ctx_flip(send, bit), FLAGS + at, group)
-    got, parts = tie(ctx_flip(send, Z1), project(numbers, own_tokens, other_tokens, weight))
-    own_part, part = parts
-    keep, send = merge(numbers, keep, send, got, FLAGS + 3, 8)
-    got, got_part = tie(ctx_flip(send, Z2), swap_core(part))
+    got, parts = tie(ctx_flip(send, Z2), project(numbers, tokens, weight, 0, 512))
+    own_early, part = parts
     keep, send = merge(numbers, keep, send, got, FLAGS + 4, 8)
-    answer, mine = merge(numbers, keep, send, ctx_flip(send, Z4))
+    got, got_early, parts = tie(ctx_flip(send, Z4), swap_core(part), project(numbers, tokens, weight, 2, 512))
+    own_late, part = parts
+    got_late = swap_core(part)
+    answer, mine = merge(numbers, keep, send, got)
     context = context_attention(
-        numbers, own_part, got_part, query_lift, cosine, sine, pair, mine, swap_core(mine)
+        numbers,
+        (own_early, got_early),
+        (own_late, got_late),
+        low,
+        query_up,
+        cosine,
+        sine,
+        pair,
+        mine,
+        swap_core(mine),
     )
     return (context, answer)
 

time: 221 us -> 197 us (0.89)
  waiting for transfers between devices: 101 us -> 75.2 us
  starting transfers between devices: 31.7 us -> 39.5 us
  local copies, waits for them, and re-layouts: 17.9 us -> 14 us
  Pallas kernels: 38.6 us -> 41.3 us
    ppermute x6, waiting for transfers between devices: 44.1 us -> 29.9 us  [ctx_flip(): return lax.ppermute(value, 'ctx', [(i, i ^ bit) for i in range(64)])]
    ppermute x2 -> x0, waiting for transfers between devices: 13.8 us -> none  [the longest x1 13.8 us: shards(): low = low + lax.ppermute(low, 'tp', [(i, i ^ 1) for i in range(YS)])]
    ppermute x6, starting transfers between devices: 6.03 us -> 11.7 us  [ctx_flip(): return lax.ppermute(value, 'ctx', [(i, i ^ bit) for i in range(64)])]
    unnamed x62 -> x46, local copies, waits for them, and re-layouts: 11.5 us -> 6.13 us
    all_gather x2, waiting for transfers between devices: 10.5 us -> 15.2 us  [gather_z(): lax.all_gather(value, 'ctx', axis_index_groups=lines, axis=0, tiled=True)]
    pallas_call x2 -> x3, Pallas kernels: 15.3 us -> 18.9 us  [project(): call(project_kernel, 4 * ROWS * 4096 * cols, 2 * 4096 * (2 * ROWS + cols)...]
    ppermute x6, starting transfers between devices: 6.42 us -> 8.63 us  [move_y(): return lax.ppermute(value, 'tp', [(y, (y + dy) % YS) for y in range(YS)])]
    ppermute x12 -> x13, waiting for transfers between devices: 24.6 us -> 23.2 us  [ctx_move(): return lax.ppermute(value, 'ctx', pairs)]
  transfers between devices with their start and end apart: 28 -> 27, of which waited for: 17 -> 17; matrix products, arithmetic and copies ran while one was open for 7% -> 7% of each run, Pallas kernels for 12% -> 16%
where the time goes in v1:
time: 197 us; the launch traced here: 195 us
  waiting for transfers between devices  75.2 us (38%)
  Pallas kernels  41.3 us (21%)
  starting transfers between devices  39.5 us (20%)
  between operations  18.8 us (10%)
  local copies, waits for them, and re-layouts  14 us (7%)
  other arithmetic  6.64 us (3%)
    ppermute x6, waiting for transfers between devices, ctx_flip(): return lax.ppermute(value, 'ctx', [(i, i ^ bit) for i in range(64)])  29.9 us
    ppermute x13, waiting for transfers between devices, ctx_move(): return lax.ppermute(value, 'ctx', pairs)  23.2 us
    ppermute x13, starting transfers between devices, ctx_move(): return lax.ppermute(value, 'ctx', pairs)  19 us
    pallas_call x3, Pallas kernels, project(): call(project_kernel, 4 * ROWS * 4096 * cols, 2 * 4096 * (2 * ROWS + cols)...  18.9 us
    all_gather x2, waiting for transfers between devices, gather_z(): lax.all_gather(value, 'ctx', axis_index_groups=lines, axis=0, tiled=True)  15.2 us
    ppermute x6, starting transfers between devices, ctx_flip(): return lax.ppermute(value, 'ctx', [(i, i ^ bit) for i in range(64)])  11.7 us
    pallas_call x1, Pallas kernels, context_attention(): call(context_kernel, 64 * ROWS * ROWS * HEAD, ROWS * 1024 * 14, 16 * ROWS...  10.1 us
    ppermute x6, starting transfers between devices, move_y(): return lax.ppermute(value, 'tp', [(y, (y + dy) % YS) for y in range(YS)])  8.63 us
  transfers between devices with their start and end apart: 27, of which 17 were waited for; matrix products, arithmetic and copies ran while one was open for 7% of the time, Pallas kernels for 16%

profile of v1, /device:TPU:1, one launch (start us, length us, event | category | flops | bytes accessed | tf_op | source)
XLA Modules:
  0.0 195.4 jit_solution(14600353438320328066)
XLA Ops:
  7.2 3.3 %collective-permute-start = (bf16[32,256]{1,0:T(8,128)(2,1)}, bf16[32,256]{1,0:T(8,128)(2,1)S(1)}, u32[]{:S(2)}, u32[]{:S(2)}) collective-permute-start(bf16[32,256]{1,0:T(8,128)(2,1)} %bitcast.35), channel_id=1, source_target_pairs={{0,4},{4,0},{8,12},{12,8},{16,20},{20,16},{24,28},{28,24},{32,36},... | collective-permute-start | bytes 49160 | tf_op jit(solution)/shard_map/ppermute | solution.py:38
  14.9 2.7 %collective-permute-start.3 = (bf16[448,1024]{1,0:T(8,128)(2,1)S(1)}, bf16[448,1024]{1,0:T(8,128)(2,1)}, u32[]{:S(2)}, u32[]{:S(2)}) collective-permute-start(bf16[448,1024]{1,0:T(8,128)(2,1)S(1)} %collective-permute-done.1.refs_4_), channel_id=1, source_target_pairs={{0,3},{1,0},{2,1},{3,2},{4,7},{5,4},{6,5},{7,6},{8,11},{9,8},{10,9... | collective-permute-start | bytes 2752520 | tf_op jit(solution)/shard_map/ppermute | solution.py:55
  29.6 4.4 %collective-permute-done.4 = bf16[128,1024]{1,0:T(8,128)(2,1)} collective-permute-done((bf16[128,1024]{1,0:T(8,128)(2,1)}, bf16[128,1024]{1,0:T(8,128)(2,1)}, u32[]{:S(2)}, u32[]{:S(2)}) %collective-permute-start.4) | collective-permute-done | bytes 262176 | tf_op jit(solution)/shard_map/ppermute | solution.py:38
  34.1 2.2 %pad_maximum_fusion.1 = bf16[4,128,1024]{2,1,0:T(8,128)(2,1)} fusion(bf16[1,128,1024]{2,1,0:T(8,128)(2,1)} %bitcast.18, bf16[1,128,1024]{2,1,0:T(8,128)(2,1)} %bitcast.17, bf16[1,128,1024]{2,1,0:T(8,128)(2,1)} %bitcast.16, bf16[1,128,1024]{2,1,0:T(8,128)(2,1)S(1)} %bitcast.34), kind=kLoop, calls=%fused_computation.1 | loop fusion | flops 1572864 | bytes 2097152 | tf_op jit(solution)/shard_map/stack | solution.py:460
  38.9 11.0 %all-gather.5.cloned.1.call-done = bf16[2048,256]{1,0:T(8,128)(2,1)} async-done(((bf16[256,256]{1,0:T(8,128)(2,1)}), bf16[2048,256]{1,0:T(8,128)(2,1)}) %all-gather.5.cloned.1.call-update) | async-done | bytes 1048592 | tf_op jit(solution)/shard_map/all_gather | solution.py:51
  53.0 2.5 %slice_bitcast_fusion = (bf16[1,8,192,256]{3,2,1,0:T(8,128)(2,1)}, bf16[8,192,256]{2,1,0:T(8,128)(2,1)}) fusion(bf16[8,256,256]{2,1,0:T(8,128)(2,1)} %bitcast.33), kind=kLoop, calls=%fused_computation.13 | loop fusion | bytes 2359296 | tf_op jit(solution)/shard_map/stack | solution.py:487
  60.0 11.2 %collective-permute-done.9 = bf16[8,192,256]{2,1,0:T(8,128)(2,1)} collective-permute-done((bf16[8,192,256]{2,1,0:T(8,128)(2,1)}, bf16[8,192,256]{2,1,0:T(8,128)(2,1)}, u32[]{:S(2)}, u32[]{:S(2)}) %collective-permute-start.9) | collective-permute-done | bytes 786464 | tf_op jit(solution)/shard_map/ppermute | solution.py:38
  73.1 2.6 %collective-permute-start.14 = (bf16[448,1024]{1,0:T(8,128)(2,1)}, bf16[448,1024]{1,0:T(8,128)(2,1)S(1)}, u32[]{:S(2)}, u32[]{:S(2)}) collective-permute-start(bf16[448,1024]{1,0:T(8,128)(2,1)} %collective-permute-done.3.refs_7_), channel_id=1, source_target_pairs={{0,3},{1,0},{2,1},{3,2},{4,7},{5,4},{6,5},{7,6},{8,11},{9,8},{10,9... | collective-permute-start | bytes 2752520 | tf_op jit(solution)/shard_map/ppermute | solution.py:55
  78.7 2.1 %collective-permute-start.12 = (bf16[4,192,256]{2,1,0:T(8,128)(2,1)S(1)}, bf16[4,192,256]{2,1,0:T(8,128)(2,1)S(1)}, u32[]{:S(2)}, u32[]{:S(2)}) collective-permute-start(bf16[4,192,256]{2,1,0:T(8,128)(2,1)S(1)} %slice.11), channel_id=1, source_target_pairs={{0,192},{4,196},{8,200},{12,204},{16,208},{20,212},{24,216},{28,22... | collective-permute-start | bytes 1179656 | tf_op jit(solution)/shard_map/ppermute | solution.py:38
  81.8 3.3 %collective-permute-done.11 = bf16[4,192,256]{2,1,0:T(8,128)(2,1)S(1)} collective-permute-done((bf16[4,192,256]{2,1,0:T(8,128)(2,1)S(1)}, bf16[4,192,256]{2,1,0:T(8,128)(2,1)S(1)}, u32[]{:S(2)}, u32[]{:S(2)}) %collective-permute-start.11) | collective-permute-done | bytes 393248 | tf_op jit(solution)/shard_map/ppermute | solution.py:38
  87.9 2.1 %collective-permute-done.14.refs_6_ = bf16[448,1024]{1,0:T(8,128)(2,1)S(1)} collective-permute-done((bf16[448,1024]{1,0:T(8,128)(2,1)}, bf16[448,1024]{1,0:T(8,128)(2,1)S(1)}, u32[]{:S(2)}, u32[]{:S(2)}) %collective-permute-start.14) | collective-permute-done | bytes 917536 | tf_op jit(solution)/shard_map/ppermute | solution.py:55
  90.0 2.9 %collective-permute-done.13.refs_2_ = bf16[448,1152]{1,0:T(8,128)(2,1)} collective-permute-done((bf16[448,1152]{1,0:T(8,128)(2,1)S(1)}, bf16[448,1152]{1,0:T(8,128)(2,1)}, u32[]{:S(2)}, u32[]{:S(2)}) %collective-permute-start.13) | collective-permute-done | bytes 1032224 | tf_op jit(solution)/shard_map/ppermute | solution.py:55
  92.9 3.7 %shard_map.124 = (f32[448,256]{1,0:T(8,128)S(1)}, f32[448,256]{1,0:T(8,128)S(1)}, bf16[448,128]{1,0:T(8,128)(2,1)S(1)}) custom-call(s32[10]{0:T(128)S(1)} %stack.67.number_ref, bf16[448,1152]{1,0:T(8,128)(2,1)S(1)} %shard_map.123.refs_0_, bf16[448,1152]{1,0:T(8,128)(2,1)S(1)} %collective-permute-done.7.refs_1_, ...), custom_call_target="tpu_custom_call" | custom-call | flops 1879048192 | bytes 10354688 | tf_op jit(solution)/shard_map/pallas_call | solution.py:181
  96.6 6.1 %collective-permute-start.15 = (f32[448,256]{1,0:T(8,128)S(1)}, f32[448,256]{1,0:T(8,128)S(1)}, u32[]{:S(2)}, u32[]{:S(2)}) collective-permute-start(f32[448,256]{1,0:T(8,128)S(1)} %get-tuple-element.60), channel_id=1, source_target_pairs={{0,4},{4,0},{8,12},{12,8},{16,20},{20,16},{24,28},{28,24},{32,36},... | collective-permute-start | bytes 1376264 | tf_op jit(solution)/shard_map/ppermute | solution.py:38
  104.2 3.7 %shard_map.125 = (f32[256,1152]{1,0:T(8,128)S(1)}, bf16[384,1152]{1,0:T(8,128)(2,1)S(1)}, bf16[448,256]{1,0:T(8,128)(2,1)S(1)}) custom-call(s32[10]{0:T(128)S(1)} %stack.67.number_ref, bf16[4,8,192,256]{3,2,1,0:T(8,128)(2,1)S(1)} %pad_maximum_fusion.refs_8_.lines_ref, f32[448,256]{1,0:T(8,128)S(1)} %get-tuple-element.59.own_ref, ...), custom_call_target="tpu_custom_call" | custom-call | flops 939524096 | bytes 3145728 | tf_op jit(solution)/shard_map/pallas_call | solution.py:384
  113.0 10.5 %collective-permute-done.17.got_ref = bf16[192,1152]{1,0:T(8,128)(2,1)S(1)} collective-permute-done((bf16[192,1152]{1,0:T(8,128)(2,1)S(1)}, bf16[192,1152]{1,0:T(8,128)(2,1)S(1)}, u32[]{:S(2)}, u32[]{:S(2)}) %collective-permute-start.17) | collective-permute-done | bytes 442400 | tf_op jit(solution)/shard_map/ppermute | solution.py:42
  124.5 2.8 %collective-permute-start.18 = (bf16[128,1152]{1,0:T(8,128)(2,1)S(1)}, bf16[128,1152]{1,0:T(8,128)(2,1)S(1)}, u32[]{:S(2)}, u32[]{:S(2)}) collective-permute-start(bf16[128,1152]{1,0:T(8,128)(2,1)S(1)} %get-tuple-element.70.sent_ref), channel_id=1, source_target_pairs={{0,128},{4,132},{8,136},{12,140},{16,144},{20,148},{24,152},{28,15... | collective-permute-start | bytes 884744 | tf_op jit(solution)/shard_map/ppermute | solution.py:42
  127.3 6.2 %collective-permute-done.18.got_ref = bf16[128,1152]{1,0:T(8,128)(2,1)S(1)} collective-permute-done((bf16[128,1152]{1,0:T(8,128)(2,1)S(1)}, bf16[128,1152]{1,0:T(8,128)(2,1)S(1)}, u32[]{:S(2)}, u32[]{:S(2)}) %collective-permute-start.18) | collective-permute-done | bytes 294944 | tf_op jit(solution)/shard_map/ppermute | solution.py:42
  134.7 11.2 %collective-permute-done.19.got_ref = bf16[96,1152]{1,0:T(8,128)(2,1)S(1)} collective-permute-done((bf16[96,1152]{1,0:T(8,128)(2,1)S(1)}, bf16[96,1152]{1,0:T(8,128)(2,1)S(1)}, u32[]{:S(2)}, u32[]{:S(2)}) %collective-permute-start.19) | collective-permute-done | bytes 221216 | tf_op jit(solution)/shard_map/ppermute | solution.py:42
  147.8 4.2 %all-gather.7.cloned.1.call-done = bf16[32,128,1024]{2,1,0:T(8,128)(2,1)} async-done(((bf16[4,128,1024]{2,1,0:T(8,128)(2,1)}), bf16[32,128,1024]{2,1,0:T(8,128)(2,1)}) %all-gather.7.cloned.1.call-update) | async-done | bytes 8388624 | tf_op jit(solution)/shard_map/all_gather | solution.py:51
  152.0 7.6 %shard_map.130 = (f32[448,512]{1,0:T(8,128)S(1)}, f32[448,512]{1,0:T(8,128)S(1)}) custom-call(s32[10]{0:T(128)S(1)} %stack.67.number_ref, bf16[448,1152]{1,0:T(8,128)(2,1)} %copy-done.1, bf16[448,1152]{1,0:T(8,128)(2,1)} %copy-done.2, bf16[448,1152]{1,0:T(8,128)(2,1)} %collective-permute-done.13.refs_2_, bf16[448,1152]{1,0:T(8,128)(2,1)} %copy-done.3, ...), custom_call_target="tpu_custom_call" | custom-call | flops 3758096384 | bytes 13369344 | tf_op jit(solution)/shard_map/pallas_call | solution.py:181
  161.7 5.9 %collective-permute-start.21 = (bf16[80,1152]{1,0:T(8,128)(2,1)S(1)}, bf16[80,1152]{1,0:T(8,128)(2,1)S(1)}, u32[]{:S(2)}, u32[]{:S(2)}) collective-permute-start(bf16[80,1152]{1,0:T(8,128)(2,1)S(1)} %get-tuple-element.80.sent_ref), channel_id=1, source_target_pairs={{0,32},{4,36},{8,40},{12,44},{16,48},{20,52},{24,56},{28,60},{32,0... | collective-permute-start | bytes 552968 | tf_op jit(solution)/shard_map/ppermute | solution.py:42
  167.5 7.6 %shard_map.132 = (f32[448,512]{1,0:T(8,128)S(1)}, f32[448,512]{1,0:T(8,128)S(1)}) custom-call(s32[10]{0:T(128)S(1)} %stack.67.number_ref, bf16[448,1152]{1,0:T(8,128)(2,1)} %copy-done.1, bf16[448,1152]{1,0:T(8,128)(2,1)} %copy-done.2, bf16[448,1152]{1,0:T(8,128)(2,1)} %collective-permute-done.13.refs_2_, bf16[448,1152]{1,0:T(8,128)(2,1)} %copy-done.3, ...), custom_call_target="tpu_custom_call" | custom-call | flops 3758096384 | bytes 13369344 | tf_op jit(solution)/shard_map/pallas_call | solution.py:181
  178.4 10.1 %shard_map.134 = bf16[448,1024]{1,0:T(8,128)(2,1)} custom-call(s32[10]{0:T(128)S(1)} %stack.67.number_ref, f32[448,512]{1,0:T(8,128)S(1)} %get-tuple-element.77.own_ref, f32[448,512]{1,0:T(8,128)S(1)} %collective-permute-done.22.got_ref, f32[448,512]{1,0:T(8,128)S(1)} %get-tuple-element.85.own_late_ref, f32[448,512]{1,0:T(8,128)S(1)} %collective-permute-done.23.got_late_ref, ...), custom_call_target="tpu_custom_call" | custom-call | flops 1644167168 | bytes 6422528 | tf_op jit(solution)/shard_map/pallas_call | solution.py:263
  (111 shorter events, 46.7 us)
Async XLA Ops:
  7.2 42.7 %all-gather.5.cloned.1.call-start = ((), (), s32[]{:S(2)}) async-start(), calls=%async_computation | async-start | bytes 1179648 | tf_op jit(solution)/shard_map/all_gather | solution.py:51
  7.2 5.3 %collective-permute-start = (bf16[32,256]{1,0:T(8,128)(2,1)}, bf16[32,256]{1,0:T(8,128)(2,1)S(1)}, u32[]{:S(2)}, u32[]{:S(2)}) collective-permute-start(bf16[32,256]{1,0:T(8,128)(2,1)} %bitcast.35), channel_id=1, source_target_pairs={{0,4},{4,0},{8,12},{12,8},{16,20},{20,16},{24,28},{28,24},{32,36},... | collective-permute-start | bytes 49160 | tf_op jit(solution)/shard_map/ppermute | solution.py:38
  14.1 137.9 %all-gather.7.cloned.1.call-start = ((), (), s32[]{:S(2)}) async-start(), calls=%async_computation.1 | async-start | bytes 9437184 | tf_op jit(solution)/shard_map/all_gather | solution.py:51
  14.9 23.0 %collective-permute-start.2 = (bf16[448,1024]{1,0:T(8,128)(2,1)S(1)}, bf16[448,1024]{1,0:T(8,128)(2,1)S(1)}, u32[]{:S(2)}, u32[]{:S(2)}) collective-permute-start(bf16[448,1024]{1,0:T(8,128)(2,1)S(1)} %collective-permute-done.1.refs_4_), channel_id=1, source_target_pairs={{0,1},{1,2},{2,3},{3,0},{4,5},{5,6},{6,7},{7,4},{8,9},{9,10},{10,1... | collective-permute-start | bytes 2752520 | tf_op jit(solution)/shard_map/ppermute | solution.py:55
  14.9 24.0 %collective-permute-start.3 = (bf16[448,1024]{1,0:T(8,128)(2,1)S(1)}, bf16[448,1024]{1,0:T(8,128)(2,1)}, u32[]{:S(2)}, u32[]{:S(2)}) collective-permute-start(bf16[448,1024]{1,0:T(8,128)(2,1)S(1)} %collective-permute-done.1.refs_4_), channel_id=1, source_target_pairs={{0,3},{1,0},{2,1},{3,2},{4,7},{5,4},{6,5},{7,6},{8,11},{9,8},{10,9... | collective-permute-start | bytes 2752520 | tf_op jit(solution)/shard_map/ppermute | solution.py:55
  17.6 12.0 %collective-permute-start.6 = (bf16[128,1024]{1,0:T(8,128)(2,1)}, bf16[128,1024]{1,0:T(8,128)(2,1)}, u32[]{:S(2)}, u32[]{:S(2)}) collective-permute-start(bf16[128,1024]{1,0:T(8,128)(2,1)} %param.13), channel_id=1, source_target_pairs={{0,192},{4,196},{8,200},{12,204},{16,208},{20,212},{24,216},{28,22... | collective-permute-start | bytes 786440 | tf_op jit(solution)/shard_map/ppermute | solution.py:38
  18.4 11.2 %collective-permute-start.5 = (bf16[128,1024]{1,0:T(8,128)(2,1)}, bf16[128,1024]{1,0:T(8,128)(2,1)}, u32[]{:S(2)}, u32[]{:S(2)}) collective-permute-start(bf16[128,1024]{1,0:T(8,128)(2,1)} %param.13), channel_id=1, source_target_pairs={{0,128},{4,132},{8,136},{12,140},{16,144},{20,148},{24,152},{28,15... | collective-permute-start | bytes 786440 | tf_op jit(solution)/shard_map/ppermute | solution.py:38
  18.9 15.1 %collective-permute-start.4 = (bf16[128,1024]{1,0:T(8,128)(2,1)}, bf16[128,1024]{1,0:T(8,128)(2,1)}, u32[]{:S(2)}, u32[]{:S(2)}) collective-permute-start(bf16[128,1024]{1,0:T(8,128)(2,1)} %param.13), channel_id=1, source_target_pairs={{0,64},{4,68},{8,72},{12,76},{16,80},{20,84},{24,88},{28,92},{32,9... | collective-permute-start | bytes 786440 | tf_op jit(solution)/shard_map/ppermute | solution.py:38
  49.9 21.6 %collective-permute-start.7 = (bf16[448,1152]{1,0:T(8,128)(2,1)S(1)}, bf16[448,1152]{1,0:T(8,128)(2,1)S(1)}, u32[]{:S(2)}, u32[]{:S(2)}) collective-permute-start(bf16[448,1152]{1,0:T(8,128)(2,1)S(1)} %shard_map.123.refs_0_), channel_id=1, source_target_pairs={{0,1},{1,2},{2,3},{3,0},{4,5},{5,6},{6,7},{7,4},{8,9},{9,10},{10,1... | collective-permute-start | bytes 3096584 | tf_op jit(solution)/shard_map/ppermute | solution.py:55
  51.1 20.4 %collective-permute-start.8 = (bf16[448,1152]{1,0:T(8,128)(2,1)S(1)}, bf16[448,1152]{1,0:T(8,128)(2,1)S(1)}, u32[]{:S(2)}, u32[]{:S(2)}) collective-permute-start(bf16[448,1152]{1,0:T(8,128)(2,1)S(1)} %shard_map.123.refs_0_), channel_id=1, source_target_pairs={{0,3},{1,0},{2,1},{3,2},{4,7},{5,4},{6,5},{7,6},{8,11},{9,8},{10,9... | collective-permute-start | bytes 3096584 | tf_op jit(solution)/shard_map/ppermute | solution.py:55
  55.5 15.7 %collective-permute-start.9 = (bf16[8,192,256]{2,1,0:T(8,128)(2,1)}, bf16[8,192,256]{2,1,0:T(8,128)(2,1)}, u32[]{:S(2)}, u32[]{:S(2)}) collective-permute-start(bf16[8,192,256]{2,1,0:T(8,128)(2,1)} %get-tuple-element.93), channel_id=1, source_target_pairs={{0,64},{4,68},{8,72},{12,76},{16,80},{20,84},{24,88},{28,92},{32,9... | collective-permute-start | bytes 2359304 | tf_op jit(solution)/shard_map/ppermute | solution.py:38
  56.5 14.7 %collective-permute-start.10 = (bf16[8,192,256]{2,1,0:T(8,128)(2,1)}, bf16[8,192,256]{2,1,0:T(8,128)(2,1)}, u32[]{:S(2)}, u32[]{:S(2)}) collective-permute-start(bf16[8,192,256]{2,1,0:T(8,128)(2,1)} %get-tuple-element.93), channel_id=1, source_target_pairs={{0,192},{4,196},{8,200},{12,204},{16,208},{20,212},{24,216},{28,22... | collective-permute-start | bytes 2359304 | tf_op jit(solution)/shard_map/ppermute | solution.py:38
  71.5 21.4 %collective-permute-start.13 = (bf16[448,1152]{1,0:T(8,128)(2,1)S(1)}, bf16[448,1152]{1,0:T(8,128)(2,1)}, u32[]{:S(2)}, u32[]{:S(2)}) collective-permute-start(bf16[448,1152]{1,0:T(8,128)(2,1)S(1)} %collective-permute-done.7.refs_1_), channel_id=1, source_target_pairs={{0,1},{1,2},{2,3},{3,0},{4,5},{5,6},{6,7},{7,4},{8,9},{9,10},{10,1... | collective-permute-start | bytes 3096584 | tf_op jit(solution)/shard_map/ppermute | solution.py:55
  73.1 16.9 %collective-permute-start.14 = (bf16[448,1024]{1,0:T(8,128)(2,1)}, bf16[448,1024]{1,0:T(8,128)(2,1)S(1)}, u32[]{:S(2)}, u32[]{:S(2)}) collective-permute-start(bf16[448,1024]{1,0:T(8,128)(2,1)} %collective-permute-done.3.refs_7_), channel_id=1, source_target_pairs={{0,3},{1,0},{2,1},{3,2},{4,7},{5,4},{6,5},{7,6},{8,11},{9,8},{10,9... | collective-permute-start | bytes 2752520 | tf_op jit(solution)/shard_map/ppermute | solution.py:55
  76.7 8.5 %collective-permute-start.11 = (bf16[4,192,256]{2,1,0:T(8,128)(2,1)S(1)}, bf16[4,192,256]{2,1,0:T(8,128)(2,1)S(1)}, u32[]{:S(2)}, u32[]{:S(2)}) collective-permute-start(bf16[4,192,256]{2,1,0:T(8,128)(2,1)S(1)} %slice.10), channel_id=1, source_target_pairs={{0,64},{4,68},{8,72},{12,76},{16,80},{20,84},{24,88},{28,92},{32,9... | collective-permute-start | bytes 1179656 | tf_op jit(solution)/shard_map/ppermute | solution.py:38
  78.7 7.4 %collective-permute-start.12 = (bf16[4,192,256]{2,1,0:T(8,128)(2,1)S(1)}, bf16[4,192,256]{2,1,0:T(8,128)(2,1)S(1)}, u32[]{:S(2)}, u32[]{:S(2)}) collective-permute-start(bf16[4,192,256]{2,1,0:T(8,128)(2,1)S(1)} %slice.11), channel_id=1, source_target_pairs={{0,192},{4,196},{8,200},{12,204},{16,208},{20,212},{24,216},{28,22... | collective-permute-start | bytes 1179656 | tf_op jit(solution)/shard_map/ppermute | solution.py:38
  96.6 7.6 %collective-permute-start.15 = (f32[448,256]{1,0:T(8,128)S(1)}, f32[448,256]{1,0:T(8,128)S(1)}, u32[]{:S(2)}, u32[]{:S(2)}) collective-permute-start(f32[448,256]{1,0:T(8,128)S(1)} %get-tuple-element.60), channel_id=1, source_target_pairs={{0,4},{4,0},{8,12},{12,8},{16,20},{20,16},{24,28},{28,24},{32,36},... | collective-permute-start | bytes 1376264 | tf_op jit(solution)/shard_map/ppermute | solution.py:38
  111.9 11.6 %collective-permute-start.17 = (bf16[192,1152]{1,0:T(8,128)(2,1)S(1)}, bf16[192,1152]{1,0:T(8,128)(2,1)S(1)}, u32[]{:S(2)}, u32[]{:S(2)}) collective-permute-start(bf16[192,1152]{1,0:T(8,128)(2,1)S(1)} %get-tuple-element.68.sent_ref), channel_id=1, source_target_pairs={{0,64},{4,68},{8,72},{12,76},{16,80},{20,84},{24,88},{28,92},{32,9... | collective-permute-start | bytes 1327112 | tf_op jit(solution)/shard_map/ppermute | solution.py:42
  124.5 9.0 %collective-permute-start.18 = (bf16[128,1152]{1,0:T(8,128)(2,1)S(1)}, bf16[128,1152]{1,0:T(8,128)(2,1)S(1)}, u32[]{:S(2)}, u32[]{:S(2)}) collective-permute-start(bf16[128,1152]{1,0:T(8,128)(2,1)S(1)} %get-tuple-element.70.sent_ref), channel_id=1, source_target_pairs={{0,128},{4,132},{8,136},{12,140},{16,144},{20,148},{24,152},{28,15... | collective-permute-start | bytes 884744 | tf_op jit(solution)/shard_map/ppermute | solution.py:42
  134.3 11.5 %collective-permute-start.19 = (bf16[96,1152]{1,0:T(8,128)(2,1)S(1)}, bf16[96,1152]{1,0:T(8,128)(2,1)S(1)}, u32[]{:S(2)}, u32[]{:S(2)}) collective-permute-start(bf16[96,1152]{1,0:T(8,128)(2,1)S(1)} %get-tuple-element.72.sent_ref), channel_id=1, source_target_pairs={{0,8},{4,12},{8,0},{12,4},{16,24},{20,28},{24,16},{28,20},{32,40},... | collective-permute-start | bytes 663560 | tf_op jit(solution)/shard_map/ppermute | solution.py:42
  146.6 13.0 %collective-permute-start.20 = (bf16[80,1152]{1,0:T(8,128)(2,1)S(1)}, bf16[80,1152]{1,0:T(8,128)(2,1)S(1)}, u32[]{:S(2)}, u32[]{:S(2)}) collective-permute-start(bf16[80,1152]{1,0:T(8,128)(2,1)S(1)} %get-tuple-element.73.sent_ref), channel_id=1, source_target_pairs={{0,16},{4,20},{8,24},{12,28},{16,0},{20,4},{24,8},{28,12},{32,48},... | collective-permute-start | bytes 552968 | tf_op jit(solution)/shard_map/ppermute | solution.py:42
  159.7 15.5 %collective-permute-start.22 = (f32[448,512]{1,0:T(8,128)S(1)}, f32[448,512]{1,0:T(8,128)S(1)}, u32[]{:S(2)}, u32[]{:S(2)}) collective-permute-start(f32[448,512]{1,0:T(8,128)S(1)} %get-tuple-element.81), channel_id=1, source_target_pairs={{0,4},{4,0},{8,12},{12,8},{16,20},{20,16},{24,28},{28,24},{32,36},... | collective-permute-start | bytes 2752520 | tf_op jit(solution)/shard_map/ppermute | solution.py:38
  161.7 13.5 %collective-permute-start.21 = (bf16[80,1152]{1,0:T(8,128)(2,1)S(1)}, bf16[80,1152]{1,0:T(8,128)(2,1)S(1)}, u32[]{:S(2)}, u32[]{:S(2)}) collective-permute-start(bf16[80,1152]{1,0:T(8,128)(2,1)S(1)} %get-tuple-element.80.sent_ref), channel_id=1, source_target_pairs={{0,32},{4,36},{8,40},{12,44},{16,48},{20,52},{24,56},{28,60},{32,0... | collective-permute-start | bytes 552968 | tf_op jit(solution)/shard_map/ppermute | solution.py:42
  175.2 3.2 %collective-permute-start.23 = (f32[448,512]{1,0:T(8,128)S(1)}, f32[448,512]{1,0:T(8,128)S(1)}, u32[]{:S(2)}, u32[]{:S(2)}) collective-permute-start(f32[448,512]{1,0:T(8,128)S(1)} %get-tuple-element.86), channel_id=1, source_target_pairs={{0,4},{4,0},{8,12},{12,8},{16,20},{20,16},{24,28},{28,24},{32,36},... | collective-permute-start | bytes 2752520 | tf_op jit(solution)/shard_map/ppermute | solution.py:38
  (26 other events, 572.3 us)
Sparse Core Ops, SparseCore 0:
  14.2 35.5 all-gather.4
  51.6 100.3 all-gather.6

commit v2 on v1

--- a/solution.py
+++ b/solution.py
@@ -12,7 +12,7 @@
 XS, ZS, YS = 4, 8, 4
 CORE, Z1, Z2, Z4, X1, X2 = 1, 2, 4, 8, 16, 32
 LINE_SENT = 256
-LINE = 192
+LINE = 160
 AROUND, BLOCK_ID, CORE_AT, PLACE_X, OWNER, FLAGS = 0, 1, 2, 3, 4, 5
 ROWS = 448
 VMEM = 32 * 1024 * 1024
@@ -299,6 +299,7 @@
 def query_kernel(
     number_ref,
     lines_ref,
+    rows_ref,
     own_ref,
     got_ref,
     low_ref,
@@ -321,7 +322,8 @@
             for pair in range(4):
                 rows = []
                 for place in (2 * pair, 2 * pair + 1):
-                    block = lines_ref[back, place, 128 + 32 * side : 160 + 32 * side].astype(F32)
+                    block = rows_ref[back, place] if side else lines_ref[back, place, 128:]
+                    block = block.astype(F32)
                     rows.append(jnp.concatenate([block[8 * g : 8 * g + 8] for g in range(4)], axis=1))
                 at = 256 * side + 64 * at_x + 16 * pair
                 query_ref[at : at + 16] = jnp.concatenate(rows, axis=0).astype(BF)
@@ -355,7 +357,8 @@
     anchor = sent_ref[:top] + got_ref[:top]
     if top == 128:
         anchor = jnp.where(number_ref[CORE_AT] == 0, anchor[:64], anchor[64:])
-    out[1][:64] = anchor
+    if group is not None:
+        out[1][:64] = anchor
     lane = lax.broadcasted_iota(jnp.int32, (rows, 128), 1)
     one, two = mine_ref[:, 1024:], unpack_terms(got_ref[top:, 1024:], 16)[:rows]
     highest = jnp.maximum(one, two)
@@ -379,7 +382,7 @@
 VMEM_BLOCK = pl.BlockSpec(memory_space=pltpu.VMEM)
 
 
-def query_attention(numbers, lines, own, got, low, up, cosine, sine):
+def query_attention(numbers, lines, rows_got, own, got, low, up, cosine, sine):
     rows = 512
     return call(
         query_kernel,
@@ -391,16 +394,16 @@
             jax.ShapeDtypeStruct((128 + rows // 2, 1152), BF),
             jax.ShapeDtypeStruct((ROWS, 256), BF),
         ),
-        in_specs=[pl.BlockSpec(memory_space=pltpu.SMEM)] + [VMEM_BLOCK] * 7,
+        in_specs=[pl.BlockSpec(memory_space=pltpu.SMEM)] + [VMEM_BLOCK] * 8,
         out_specs=(VMEM_BLOCK,) * 3,
         scratch_shapes=[pltpu.VMEM((rows, 1024), BF)],
-    )(numbers, lines, own, got, low, up, cosine, sine)
+    )(numbers, lines, rows_got, own, got, low, up, cosine, sine)
 
 
 def merge(numbers, mine, sent, got, at_flag=0, group=None):
     rows = mine.shape[0]
     if group is None:
-        shapes = (jax.ShapeDtypeStruct((rows, 1024), BF), jax.ShapeDtypeStruct((64, 1152), BF))
+        shapes = (jax.ShapeDtypeStruct((rows, 1024), BF),)
     else:
         half = rows // 2
         shapes = (
@@ -413,7 +416,7 @@
         rows * 1152 * 8,
         out_shape=shapes,
         in_specs=[pl.BlockSpec(memory_space=pltpu.SMEM)] + [VMEM_BLOCK] * 3,
-        out_specs=(VMEM_BLOCK,) * 2,
+        out_specs=(VMEM_BLOCK,) * len(shapes),
     )(numbers, mine, sent, got)
 
 
@@ -452,7 +455,7 @@
     packed = query_rows.reshape(8, 4, 256).transpose(1, 0, 2).reshape(32, 256)
     blank = jnp.zeros((LINE_SENT - LINE, 256), BF)
     line = jnp.concatenate(
-        [jnp.concatenate([key_weight, value_weight], axis=1), packed, swap_core(packed), blank], axis=0
+        [jnp.concatenate([key_weight, value_weight], axis=1), packed, blank], axis=0
     )
     line = gather_z(line[None])
     other = swap_core(theirs_of(core, hidden))
@@ -486,7 +489,7 @@
     far, cosine, sine, value_up = tie(far, cosine, sine, value_up)
     lines = jnp.stack([line, ahead, jnp.concatenate(far, axis=0), behind])
     own_part, part, low = project(numbers, tokens, lines)
-    keep, send, pair = query_attention(numbers, lines, own_part, swap_core(part), low, value_up, cosine, sine)
+    keep, send, pair = query_attention(numbers, lines, swap_core(lines[:, :, 128:]), own_part, swap_core(part), low, value_up, cosine, sine)
     for bit, at, group in ((CORE, 0, 64), (X1, 1, 64), (X2, 2, 8), (Z1, 3, 8)):
         keep, send = merge(numbers, keep, send, ctx_flip(send, bit), FLAGS + at, group)
     got, parts = tie(ctx_flip(send, Z2), project(numbers, tokens, weight, 0, 512))
@@ -495,7 +498,8 @@
     got, got_early, parts = tie(ctx_flip(send, Z4), swap_core(part), project(numbers, tokens, weight, 2, 512))
     own_late, part = parts
     got_late = swap_core(part)
-    answer, mine = merge(numbers, keep, send, got)
+    mine = send[:64] + got[:64]
+    (answer,) = merge(numbers, keep, send, got)
     context = context_attention(
         numbers,
         (own_early, got_early),

time: 197 us -> 196 us (level)
  waiting for transfers between devices: 75.2 us -> 68.6 us
  starting transfers between devices: 39.5 us -> 45.2 us
    ppermute x13, starting transfers between devices: 19 us -> 24.4 us  [ctx_move(): return lax.ppermute(value, 'ctx', pairs)]
    ppermute x13, waiting for transfers between devices: 23.2 us -> 19.2 us  [ctx_move(): return lax.ppermute(value, 'ctx', pairs)]
    ppermute x6, waiting for transfers between devices: 6.9 us -> 4.89 us  [move_y(): return lax.ppermute(value, 'tp', [(y, (y + dy) % YS) for y in range(YS)])]
    unnamed x46 -> x54, local copies, waits for them, and re-layouts: 6.13 us -> 6.17 us
  transfers between devices with their start and end apart: 27 -> 27, of which waited for: 17 -> 16; matrix products, arithmetic and copies ran while one was open for 7% -> 7% of each run, Pallas kernels for 16% -> 16%
where the time goes in v2:
time: 196 us; the launch traced here: 194 us
  waiting for transfers between devices  68.6 us (35%)
  starting transfers between devices  45.2 us (23%)
  Pallas kernels  41.6 us (21%)
  between operations  18.9 us (10%)
  local copies, waits for them, and re-layouts  13.9 us (7%)
  other arithmetic  5.89 us (3%)
    ppermute x6, waiting for transfers between devices, ctx_flip(): return lax.ppermute(value, 'ctx', [(i, i ^ bit) for i in range(64)])  29.8 us
    ppermute x13, starting transfers between devices, ctx_move(): return lax.ppermute(value, 'ctx', pairs)  24.4 us
    pallas_call x3, Pallas kernels, project(): call(project_kernel, 4 * ROWS * 4096 * cols, 2 * 4096 * (2 * ROWS + cols)...  19.2 us
    ppermute x13, waiting for transfers between devices, ctx_move(): return lax.ppermute(value, 'ctx', pairs)  19.2 us
    all_gather x2, waiting for transfers between devices, gather_z(): lax.all_gather(value, 'ctx', axis_index_groups=lines, axis=0, tiled=True)  14.6 us
    ppermute x6, starting transfers between devices, ctx_flip(): return lax.ppermute(value, 'ctx', [(i, i ^ bit) for i in range(64)])  12.4 us
    pallas_call x1, Pallas kernels, context_attention(): call(context_kernel, 64 * ROWS * ROWS * HEAD, ROWS * 1024 * 14, 16 * ROWS...  10.1 us
    ppermute x6, starting transfers between devices, move_y(): return lax.ppermute(value, 'tp', [(y, (y + dy) % YS) for y in range(YS)])  8.25 us
  transfers between devices with their start and end apart: 27, of which 16 were waited for; matrix products, arithmetic and copies ran while one was open for 7% of the time, Pallas kernels for 16%

profile of v2, /device:TPU:1, one launch (start us, length us, event | category | flops | bytes accessed | tf_op | source)
XLA Modules:
  0.0 194.0 jit_solution(13621098042587271192)
XLA Ops:
  9.1 3.3 %collective-permute-start = (bf16[448,1024]{1,0:T(8,128)(2,1)S(1)}, bf16[448,1024]{1,0:T(8,128)(2,1)S(1)}, u32[]{:S(2)}, u32[]{:S(2)}) collective-permute-start(bf16[448,1024]{1,0:T(8,128)(2,1)S(1)} %shard_map.122), channel_id=1, source_target_pairs={{0,4},{4,0},{8,12},{12,8},{16,20},{20,16},{24,28},{28,24},{32,36},... | collective-permute-start | bytes 2752520 | tf_op jit(solution)/shard_map/ppermute | solution.py:38
  14.5 2.7 %collective-permute-start.2 = (bf16[448,1024]{1,0:T(8,128)(2,1)S(1)}, bf16[448,1024]{1,0:T(8,128)(2,1)}, u32[]{:S(2)}, u32[]{:S(2)}) collective-permute-start(bf16[448,1024]{1,0:T(8,128)(2,1)S(1)} %collective-permute-done.refs_4_), channel_id=1, source_target_pairs={{0,3},{1,0},{2,1},{3,2},{4,7},{5,4},{6,5},{7,6},{8,11},{9,8},{10,9... | collective-permute-start | bytes 2752520 | tf_op jit(solution)/shard_map/ppermute | solution.py:55
  27.3 2.0 %shard_map.123.refs_0_ = bf16[448,1152]{1,0:T(8,128)(2,1)S(1)} custom-call(s32[10]{0:T(128)S(1)} %stack.67.number_ref, bf16[448,2048]{1,0:T(8,128)(2,1)S(1)} %copy-done.13, bf16[2048,128]{1,0:T(8,128)(2,1)S(1)} %copy-done.18, bf16[2048,128]{1,0:T(8,128)(2,1)S(1)} %copy-done.19), custom_call_target="tpu_custom_call" | custom-call | flops 469762048 | bytes 3801088 | tf_op jit(solution)/shard_map/pallas_call | solution.py:144
  29.3 4.1 %collective-permute-done.3 = bf16[128,1024]{1,0:T(8,128)(2,1)} collective-permute-done((bf16[128,1024]{1,0:T(8,128)(2,1)S(1)}, bf16[128,1024]{1,0:T(8,128)(2,1)}, u32[]{:S(2)}, u32[]{:S(2)}) %collective-permute-start.3) | collective-permute-done | bytes 262176 | tf_op jit(solution)/shard_map/ppermute | solution.py:38
  33.4 2.2 %pad_maximum_fusion.1 = bf16[4,128,1024]{2,1,0:T(8,128)(2,1)} fusion(bf16[1,128,1024]{2,1,0:T(8,128)(2,1)} %bitcast.16, bf16[1,128,1024]{2,1,0:T(8,128)(2,1)} %bitcast.15, bf16[1,128,1024]{2,1,0:T(8,128)(2,1)} %bitcast.14, bf16[1,128,1024]{2,1,0:T(8,128)(2,1)S(1)} %bitcast.34), kind=kLoop, calls=%fused_computation.1 | loop fusion | flops 1572864 | bytes 2097152 | tf_op jit(solution)/shard_map/stack | solution.py:463
  38.2 10.6 %all-gather.5.cloned.1.call-done = bf16[2048,256]{1,0:T(8,128)(2,1)} async-done(((bf16[256,256]{1,0:T(8,128)(2,1)}), bf16[2048,256]{1,0:T(8,128)(2,1)}) %all-gather.5.cloned.1.call-update) | async-done | bytes 1048592 | tf_op jit(solution)/shard_map/all_gather | solution.py:51
  51.6 2.3 %slice_bitcast_fusion = (bf16[1,8,160,256]{3,2,1,0:T(8,128)(2,1)}, bf16[8,160,256]{2,1,0:T(8,128)(2,1)}) fusion(bf16[8,256,256]{2,1,0:T(8,128)(2,1)} %bitcast.33), kind=kLoop, calls=%fused_computation.14 | loop fusion | bytes 1966080 | tf_op jit(solution)/shard_map/stack | solution.py:490
  59.1 7.3 %collective-permute-done.8 = bf16[8,160,256]{2,1,0:T(8,128)(2,1)} collective-permute-done((bf16[8,160,256]{2,1,0:T(8,128)(2,1)}, bf16[8,160,256]{2,1,0:T(8,128)(2,1)}, u32[]{:S(2)}, u32[]{:S(2)}) %collective-permute-start.8) | collective-permute-done | bytes 655392 | tf_op jit(solution)/shard_map/ppermute | solution.py:38
  66.5 3.3 %collective-permute-done.6.refs_1_ = bf16[448,1152]{1,0:T(8,128)(2,1)S(1)} collective-permute-done((bf16[448,1152]{1,0:T(8,128)(2,1)S(1)}, bf16[448,1152]{1,0:T(8,128)(2,1)S(1)}, u32[]{:S(2)}, u32[]{:S(2)}) %collective-permute-start.6) | collective-permute-done | bytes 1032224 | tf_op jit(solution)/shard_map/ppermute | solution.py:55
  79.4 2.5 %collective-permute-done.10 = bf16[4,160,256]{2,1,0:T(8,128)(2,1)S(1)} collective-permute-done((bf16[4,160,256]{2,1,0:T(8,128)(2,1)S(1)}, bf16[4,160,256]{2,1,0:T(8,128)(2,1)S(1)}, u32[]{:S(2)}, u32[]{:S(2)}) %collective-permute-start.10) | collective-permute-done | bytes 327712 | tf_op jit(solution)/shard_map/ppermute | solution.py:38
  85.7 7.6 %collective-permute-start.12 = (bf16[4,8,32,256]{3,2,1,0:T(8,128)(2,1)S(1)}, bf16[4,8,32,256]{3,2,1,0:T(8,128)(2,1)S(1)}, u32[]{:S(2)}, u32[]{:S(2)}) collective-permute-start(bf16[4,8,32,256]{3,2,1,0:T(8,128)(2,1)S(1)} %slice.24), channel_id=1, source_target_pairs={{0,4},{4,0},{8,12},{12,8},{16,20},{20,16},{24,28},{28,24},{32,36},... | collective-permute-start | bytes 1572872 | tf_op jit(solution)/shard_map/ppermute | solution.py:38
  93.4 4.0 %shard_map.124 = (f32[448,256]{1,0:T(8,128)S(1)}, f32[448,256]{1,0:T(8,128)S(1)}, bf16[448,128]{1,0:T(8,128)(2,1)S(1)}) custom-call(s32[10]{0:T(128)S(1)} %stack.67.number_ref, bf16[448,1152]{1,0:T(8,128)(2,1)S(1)} %shard_map.123.refs_0_, bf16[448,1152]{1,0:T(8,128)(2,1)S(1)} %collective-permute-done.6.refs_1_, ...), custom_call_target="tpu_custom_call" | custom-call | flops 1879048192 | bytes 10354688 | tf_op jit(solution)/shard_map/pallas_call | solution.py:181
  97.4 4.0 %collective-permute-start.15 = (f32[448,256]{1,0:T(8,128)S(1)}, f32[448,256]{1,0:T(8,128)S(1)}, u32[]{:S(2)}, u32[]{:S(2)}) collective-permute-start(f32[448,256]{1,0:T(8,128)S(1)} %get-tuple-element.58), channel_id=1, source_target_pairs={{0,4},{4,0},{8,12},{12,8},{16,20},{20,16},{24,28},{28,24},{32,36},... | collective-permute-start | bytes 1376264 | tf_op jit(solution)/shard_map/ppermute | solution.py:38
  102.8 3.7 %shard_map.125 = (f32[256,1152]{1,0:T(8,128)S(1)}, bf16[384,1152]{1,0:T(8,128)(2,1)S(1)}, bf16[448,256]{1,0:T(8,128)(2,1)S(1)}) custom-call(s32[10]{0:T(128)S(1)} %stack.67.number_ref, bf16[4,8,160,256]{3,2,1,0:T(8,128)(2,1)S(1)} %pad_maximum_fusion.refs_8_.lines_ref, bf16[4,8,32,256]{3,2,1,0:T(8,128)(2,1)S(1)} %collective-permute-done.12.rows_ref, ...), custom_call_target="tpu_custom_call" | custom-call | flops 939524096 | bytes 3145728 | tf_op jit(solution)/shard_map/pallas_call | solution.py:387
  107.0 2.1 %collective-permute-done.16.got_ref = bf16[384,1152]{1,0:T(8,128)(2,1)S(1)} collective-permute-done((bf16[384,1152]{1,0:T(8,128)(2,1)S(1)}, bf16[384,1152]{1,0:T(8,128)(2,1)S(1)}, u32[]{:S(2)}, u32[]{:S(2)}) %collective-permute-start.16) | collective-permute-done | bytes 884768 | tf_op jit(solution)/shard_map/ppermute | solution.py:42
  111.8 10.3 %collective-permute-done.17.got_ref = bf16[192,1152]{1,0:T(8,128)(2,1)S(1)} collective-permute-done((bf16[192,1152]{1,0:T(8,128)(2,1)S(1)}, bf16[192,1152]{1,0:T(8,128)(2,1)S(1)}, u32[]{:S(2)}, u32[]{:S(2)}) %collective-permute-start.17) | collective-permute-done | bytes 442400 | tf_op jit(solution)/shard_map/ppermute | solution.py:42
  123.1 3.3 %collective-permute-start.18 = (bf16[128,1152]{1,0:T(8,128)(2,1)S(1)}, bf16[128,1152]{1,0:T(8,128)(2,1)S(1)}, u32[]{:S(2)}, u32[]{:S(2)}) collective-permute-start(bf16[128,1152]{1,0:T(8,128)(2,1)S(1)} %get-tuple-element.68.sent_ref), channel_id=1, source_target_pairs={{0,128},{4,132},{8,136},{12,140},{16,144},{20,148},{24,152},{28,15... | collective-permute-start | bytes 884744 | tf_op jit(solution)/shard_map/ppermute | solution.py:42
  126.3 6.2 %collective-permute-done.18.got_ref = bf16[128,1152]{1,0:T(8,128)(2,1)S(1)} collective-permute-done((bf16[128,1152]{1,0:T(8,128)(2,1)S(1)}, bf16[128,1152]{1,0:T(8,128)(2,1)S(1)}, u32[]{:S(2)}, u32[]{:S(2)}) %collective-permute-start.18) | collective-permute-done | bytes 294944 | tf_op jit(solution)/shard_map/ppermute | solution.py:42
  133.7 11.3 %collective-permute-done.19.got_ref = bf16[96,1152]{1,0:T(8,128)(2,1)S(1)} collective-permute-done((bf16[96,1152]{1,0:T(8,128)(2,1)S(1)}, bf16[96,1152]{1,0:T(8,128)(2,1)S(1)}, u32[]{:S(2)}, u32[]{:S(2)}) %collective-permute-start.19) | collective-permute-done | bytes 221216 | tf_op jit(solution)/shard_map/ppermute | solution.py:42
  146.8 4.0 %all-gather.7.cloned.1.call-done = bf16[32,128,1024]{2,1,0:T(8,128)(2,1)} async-done(((bf16[4,128,1024]{2,1,0:T(8,128)(2,1)}), bf16[32,128,1024]{2,1,0:T(8,128)(2,1)}) %all-gather.7.cloned.1.call-update) | async-done | bytes 8388624 | tf_op jit(solution)/shard_map/all_gather | solution.py:51
  150.8 7.6 %shard_map.130 = (f32[448,512]{1,0:T(8,128)S(1)}, f32[448,512]{1,0:T(8,128)S(1)}) custom-call(s32[10]{0:T(128)S(1)} %stack.67.number_ref, bf16[448,1152]{1,0:T(8,128)(2,1)} %copy-done.1, bf16[448,1152]{1,0:T(8,128)(2,1)} %copy-done.2, bf16[448,1152]{1,0:T(8,128)(2,1)} %copy-done.4, bf16[448,1152]{1,0:T(8,128)(2,1)} %copy-done.3, ...), custom_call_target="tpu_custom_call" | custom-call | flops 3758096384 | bytes 13369344 | tf_op jit(solution)/shard_map/pallas_call | solution.py:181
  160.4 6.2 %collective-permute-start.21 = (bf16[80,1152]{1,0:T(8,128)(2,1)S(1)}, bf16[80,1152]{1,0:T(8,128)(2,1)S(1)}, u32[]{:S(2)}, u32[]{:S(2)}) collective-permute-start(bf16[80,1152]{1,0:T(8,128)(2,1)S(1)} %get-tuple-element.78.sent_ref), channel_id=1, source_target_pairs={{0,32},{4,36},{8,40},{12,44},{16,48},{20,52},{24,56},{28,60},{32,0... | collective-permute-start | bytes 552968 | tf_op jit(solution)/shard_map/ppermute | solution.py:42
  166.6 7.6 %shard_map.132 = (f32[448,512]{1,0:T(8,128)S(1)}, f32[448,512]{1,0:T(8,128)S(1)}) custom-call(s32[10]{0:T(128)S(1)} %stack.67.number_ref, bf16[448,1152]{1,0:T(8,128)(2,1)} %copy-done.1, bf16[448,1152]{1,0:T(8,128)(2,1)} %copy-done.2, bf16[448,1152]{1,0:T(8,128)(2,1)} %copy-done.4, bf16[448,1152]{1,0:T(8,128)(2,1)} %copy-done.3, ...), custom_call_target="tpu_custom_call" | custom-call | flops 3758096384 | bytes 13369344 | tf_op jit(solution)/shard_map/pallas_call | solution.py:181
  177.1 10.1 %shard_map.133 = bf16[448,1024]{1,0:T(8,128)(2,1)} custom-call(s32[10]{0:T(128)S(1)} %stack.67.number_ref, f32[448,512]{1,0:T(8,128)S(1)} %get-tuple-element.75.own_ref, f32[448,512]{1,0:T(8,128)S(1)} %collective-permute-done.22.got_ref, f32[448,512]{1,0:T(8,128)S(1)} %get-tuple-element.83.own_late_ref, f32[448,512]{1,0:T(8,128)S(1)} %collective-permute-done.23.got_late_ref, ...), custom_call_target="tpu_custom_call" | custom-call | flops 1644167168 | bytes 6422528 | tf_op jit(solution)/shard_map/pallas_call | solution.py:263
  (121 shorter events, 46.8 us)
Async XLA Ops:
  7.2 41.6 %all-gather.5.cloned.1.call-start = ((), (), s32[]{:S(2)}) async-start(), calls=%async_computation | async-start | bytes 1179648 | tf_op jit(solution)/shard_map/all_gather | solution.py:51
  9.1 5.4 %collective-permute-start = (bf16[448,1024]{1,0:T(8,128)(2,1)S(1)}, bf16[448,1024]{1,0:T(8,128)(2,1)S(1)}, u32[]{:S(2)}, u32[]{:S(2)}) collective-permute-start(bf16[448,1024]{1,0:T(8,128)(2,1)S(1)} %shard_map.122), channel_id=1, source_target_pairs={{0,4},{4,0},{8,12},{12,8},{16,20},{20,16},{24,28},{28,24},{32,36},... | collective-permute-start | bytes 2752520 | tf_op jit(solution)/shard_map/ppermute | solution.py:38
  13.3 137.5 %all-gather.7.cloned.1.call-start = ((), (), s32[]{:S(2)}) async-start(), calls=%async_computation.1 | async-start | bytes 9437184 | tf_op jit(solution)/shard_map/all_gather | solution.py:51
  14.5 22.8 %collective-permute-start.1 = (bf16[448,1024]{1,0:T(8,128)(2,1)S(1)}, bf16[448,1024]{1,0:T(8,128)(2,1)S(1)}, u32[]{:S(2)}, u32[]{:S(2)}) collective-permute-start(bf16[448,1024]{1,0:T(8,128)(2,1)S(1)} %collective-permute-done.refs_4_), channel_id=1, source_target_pairs={{0,1},{1,2},{2,3},{3,0},{4,5},{5,6},{6,7},{7,4},{8,9},{9,10},{10,1... | collective-permute-start | bytes 2752520 | tf_op jit(solution)/shard_map/ppermute | solution.py:55
  14.5 23.7 %collective-permute-start.2 = (bf16[448,1024]{1,0:T(8,128)(2,1)S(1)}, bf16[448,1024]{1,0:T(8,128)(2,1)}, u32[]{:S(2)}, u32[]{:S(2)}) collective-permute-start(bf16[448,1024]{1,0:T(8,128)(2,1)S(1)} %collective-permute-done.refs_4_), channel_id=1, source_target_pairs={{0,3},{1,0},{2,1},{3,2},{4,7},{5,4},{6,5},{7,6},{8,11},{9,8},{10,9... | collective-permute-start | bytes 2752520 | tf_op jit(solution)/shard_map/ppermute | solution.py:55
  17.2 12.1 %collective-permute-start.5 = (bf16[128,1024]{1,0:T(8,128)(2,1)S(1)}, bf16[128,1024]{1,0:T(8,128)(2,1)}, u32[]{:S(2)}, u32[]{:S(2)}) collective-permute-start(bf16[128,1024]{1,0:T(8,128)(2,1)S(1)} %copy-done.21), channel_id=1, source_target_pairs={{0,192},{4,196},{8,200},{12,204},{16,208},{20,212},{24,216},{28,22... | collective-permute-start | bytes 786440 | tf_op jit(solution)/shard_map/ppermute | solution.py:38
  18.0 11.3 %collective-permute-start.4 = (bf16[128,1024]{1,0:T(8,128)(2,1)S(1)}, bf16[128,1024]{1,0:T(8,128)(2,1)}, u32[]{:S(2)}, u32[]{:S(2)}) collective-permute-start(bf16[128,1024]{1,0:T(8,128)(2,1)S(1)} %copy-done.21), channel_id=1, source_target_pairs={{0,128},{4,132},{8,136},{12,140},{16,144},{20,148},{24,152},{28,15... | collective-permute-start | bytes 786440 | tf_op jit(solution)/shard_map/ppermute | solution.py:38
  18.5 14.9 %collective-permute-start.3 = (bf16[128,1024]{1,0:T(8,128)(2,1)S(1)}, bf16[128,1024]{1,0:T(8,128)(2,1)}, u32[]{:S(2)}, u32[]{:S(2)}) collective-permute-start(bf16[128,1024]{1,0:T(8,128)(2,1)S(1)} %copy-done.21), channel_id=1, source_target_pairs={{0,64},{4,68},{8,72},{12,76},{16,80},{20,84},{24,88},{28,92},{32,9... | collective-permute-start | bytes 786440 | tf_op jit(solution)/shard_map/ppermute | solution.py:38
  48.8 21.0 %collective-permute-start.6 = (bf16[448,1152]{1,0:T(8,128)(2,1)S(1)}, bf16[448,1152]{1,0:T(8,128)(2,1)S(1)}, u32[]{:S(2)}, u32[]{:S(2)}) collective-permute-start(bf16[448,1152]{1,0:T(8,128)(2,1)S(1)} %shard_map.123.refs_0_), channel_id=1, source_target_pairs={{0,1},{1,2},{2,3},{3,0},{4,5},{5,6},{6,7},{7,4},{8,9},{9,10},{10,1... | collective-permute-start | bytes 3096584 | tf_op jit(solution)/shard_map/ppermute | solution.py:55
  50.1 19.7 %collective-permute-start.7 = (bf16[448,1152]{1,0:T(8,128)(2,1)S(1)}, bf16[448,1152]{1,0:T(8,128)(2,1)S(1)}, u32[]{:S(2)}, u32[]{:S(2)}) collective-permute-start(bf16[448,1152]{1,0:T(8,128)(2,1)S(1)} %shard_map.123.refs_0_), channel_id=1, source_target_pairs={{0,3},{1,0},{2,1},{3,2},{4,7},{5,4},{6,5},{7,6},{8,11},{9,8},{10,9... | collective-permute-start | bytes 3096584 | tf_op jit(solution)/shard_map/ppermute | solution.py:55
  53.9 12.5 %collective-permute-start.8 = (bf16[8,160,256]{2,1,0:T(8,128)(2,1)}, bf16[8,160,256]{2,1,0:T(8,128)(2,1)}, u32[]{:S(2)}, u32[]{:S(2)}) collective-permute-start(bf16[8,160,256]{2,1,0:T(8,128)(2,1)} %get-tuple-element.89), channel_id=1, source_target_pairs={{0,64},{4,68},{8,72},{12,76},{16,80},{20,84},{24,88},{28,92},{32,9... | collective-permute-start | bytes 1966088 | tf_op jit(solution)/shard_map/ppermute | solution.py:38
  55.1 11.4 %collective-permute-start.9 = (bf16[8,160,256]{2,1,0:T(8,128)(2,1)}, bf16[8,160,256]{2,1,0:T(8,128)(2,1)}, u32[]{:S(2)}, u32[]{:S(2)}) collective-permute-start(bf16[8,160,256]{2,1,0:T(8,128)(2,1)} %get-tuple-element.89), channel_id=1, source_target_pairs={{0,192},{4,196},{8,200},{12,204},{16,208},{20,212},{24,216},{28,22... | collective-permute-start | bytes 1966088 | tf_op jit(solution)/shard_map/ppermute | solution.py:38
  69.8 23.5 %collective-permute-start.13 = (bf16[448,1152]{1,0:T(8,128)(2,1)S(1)}, bf16[448,1152]{1,0:T(8,128)(2,1)S(1)}, u32[]{:S(2)}, u32[]{:S(2)}) collective-permute-start(bf16[448,1152]{1,0:T(8,128)(2,1)S(1)} %collective-permute-done.6.refs_1_), channel_id=1, source_target_pairs={{0,1},{1,2},{2,3},{3,0},{4,5},{5,6},{6,7},{7,4},{8,9},{9,10},{10,1... | collective-permute-start | bytes 3096584 | tf_op jit(solution)/shard_map/ppermute | solution.py:55
  71.3 22.0 %collective-permute-start.14 = (bf16[448,1024]{1,0:T(8,128)(2,1)}, bf16[448,1024]{1,0:T(8,128)(2,1)S(1)}, u32[]{:S(2)}, u32[]{:S(2)}) collective-permute-start(bf16[448,1024]{1,0:T(8,128)(2,1)} %collective-permute-done.2.refs_7_), channel_id=1, source_target_pairs={{0,3},{1,0},{2,1},{3,2},{4,7},{5,4},{6,5},{7,6},{8,11},{9,8},{10,9... | collective-permute-start | bytes 2752520 | tf_op jit(solution)/shard_map/ppermute | solution.py:55
  74.3 7.6 %collective-permute-start.10 = (bf16[4,160,256]{2,1,0:T(8,128)(2,1)S(1)}, bf16[4,160,256]{2,1,0:T(8,128)(2,1)S(1)}, u32[]{:S(2)}, u32[]{:S(2)}) collective-permute-start(bf16[4,160,256]{2,1,0:T(8,128)(2,1)S(1)} %slice.19), channel_id=1, source_target_pairs={{0,64},{4,68},{8,72},{12,76},{16,80},{20,84},{24,88},{28,92},{32,9... | collective-permute-start | bytes 983048 | tf_op jit(solution)/shard_map/ppermute | solution.py:38
  76.5 7.3 %collective-permute-start.11 = (bf16[4,160,256]{2,1,0:T(8,128)(2,1)S(1)}, bf16[4,160,256]{2,1,0:T(8,128)(2,1)S(1)}, u32[]{:S(2)}, u32[]{:S(2)}) collective-permute-start(bf16[4,160,256]{2,1,0:T(8,128)(2,1)S(1)} %slice.20), channel_id=1, source_target_pairs={{0,192},{4,196},{8,200},{12,204},{16,208},{20,212},{24,216},{28,22... | collective-permute-start | bytes 983048 | tf_op jit(solution)/shard_map/ppermute | solution.py:38
  85.7 15.7 %collective-permute-start.12 = (bf16[4,8,32,256]{3,2,1,0:T(8,128)(2,1)S(1)}, bf16[4,8,32,256]{3,2,1,0:T(8,128)(2,1)S(1)}, u32[]{:S(2)}, u32[]{:S(2)}) collective-permute-start(bf16[4,8,32,256]{3,2,1,0:T(8,128)(2,1)S(1)} %slice.24), channel_id=1, source_target_pairs={{0,4},{4,0},{8,12},{12,8},{16,20},{20,16},{24,28},{28,24},{32,36},... | collective-permute-start | bytes 1572872 | tf_op jit(solution)/shard_map/ppermute | solution.py:38
  97.4 5.4 %collective-permute-start.15 = (f32[448,256]{1,0:T(8,128)S(1)}, f32[448,256]{1,0:T(8,128)S(1)}, u32[]{:S(2)}, u32[]{:S(2)}) collective-permute-start(f32[448,256]{1,0:T(8,128)S(1)} %get-tuple-element.58), channel_id=1, source_target_pairs={{0,4},{4,0},{8,12},{12,8},{16,20},{20,16},{24,28},{28,24},{32,36},... | collective-permute-start | bytes 1376264 | tf_op jit(solution)/shard_map/ppermute | solution.py:38
  110.5 11.6 %collective-permute-start.17 = (bf16[192,1152]{1,0:T(8,128)(2,1)S(1)}, bf16[192,1152]{1,0:T(8,128)(2,1)S(1)}, u32[]{:S(2)}, u32[]{:S(2)}) collective-permute-start(bf16[192,1152]{1,0:T(8,128)(2,1)S(1)} %get-tuple-element.66.sent_ref), channel_id=1, source_target_pairs={{0,64},{4,68},{8,72},{12,76},{16,80},{20,84},{24,88},{28,92},{32,9... | collective-permute-start | bytes 1327112 | tf_op jit(solution)/shard_map/ppermute | solution.py:42
  123.1 9.4 %collective-permute-start.18 = (bf16[128,1152]{1,0:T(8,128)(2,1)S(1)}, bf16[128,1152]{1,0:T(8,128)(2,1)S(1)}, u32[]{:S(2)}, u32[]{:S(2)}) collective-permute-start(bf16[128,1152]{1,0:T(8,128)(2,1)S(1)} %get-tuple-element.68.sent_ref), channel_id=1, source_target_pairs={{0,128},{4,132},{8,136},{12,140},{16,144},{20,148},{24,152},{28,15... | collective-permute-start | bytes 884744 | tf_op jit(solution)/shard_map/ppermute | solution.py:42
  133.4 11.6 %collective-permute-start.19 = (bf16[96,1152]{1,0:T(8,128)(2,1)S(1)}, bf16[96,1152]{1,0:T(8,128)(2,1)S(1)}, u32[]{:S(2)}, u32[]{:S(2)}) collective-permute-start(bf16[96,1152]{1,0:T(8,128)(2,1)S(1)} %get-tuple-element.70.sent_ref), channel_id=1, source_target_pairs={{0,8},{4,12},{8,0},{12,4},{16,24},{20,28},{24,16},{28,20},{32,40},... | collective-permute-start | bytes 663560 | tf_op jit(solution)/shard_map/ppermute | solution.py:42
  145.8 12.6 %collective-permute-start.20 = (bf16[80,1152]{1,0:T(8,128)(2,1)S(1)}, bf16[80,1152]{1,0:T(8,128)(2,1)S(1)}, u32[]{:S(2)}, u32[]{:S(2)}) collective-permute-start(bf16[80,1152]{1,0:T(8,128)(2,1)S(1)} %get-tuple-element.71.sent_ref), channel_id=1, source_target_pairs={{0,16},{4,20},{8,24},{12,28},{16,0},{20,4},{24,8},{28,12},{32,48},... | collective-permute-start | bytes 552968 | tf_op jit(solution)/shard_map/ppermute | solution.py:42
  158.4 15.8 %collective-permute-start.22 = (f32[448,512]{1,0:T(8,128)S(1)}, f32[448,512]{1,0:T(8,128)S(1)}, u32[]{:S(2)}, u32[]{:S(2)}) collective-permute-start(f32[448,512]{1,0:T(8,128)S(1)} %get-tuple-element.79), channel_id=1, source_target_pairs={{0,4},{4,0},{8,12},{12,8},{16,20},{20,16},{24,28},{28,24},{32,36},... | collective-permute-start | bytes 2752520 | tf_op jit(solution)/shard_map/ppermute | solution.py:38
  160.4 13.8 %collective-permute-start.21 = (bf16[80,1152]{1,0:T(8,128)(2,1)S(1)}, bf16[80,1152]{1,0:T(8,128)(2,1)S(1)}, u32[]{:S(2)}, u32[]{:S(2)}) collective-permute-start(bf16[80,1152]{1,0:T(8,128)(2,1)S(1)} %get-tuple-element.78.sent_ref), channel_id=1, source_target_pairs={{0,32},{4,36},{8,40},{12,44},{16,48},{20,52},{24,56},{28,60},{32,0... | collective-permute-start | bytes 552968 | tf_op jit(solution)/shard_map/ppermute | solution.py:42
  (30 other events, 576.5 us)
Sparse Core Ops, SparseCore 0:
  13.4 35.3 all-gather.4
  50.6 100.0 all-gather.6
